TPU v7x, 128 devices: a whole 4x4x4 slice. The times are simulated.
128 devices in a mesh: tm: 16 (over x, y), space: 8 (over z, core).
Axes of the slice: x: 4, y: 4, z: 4, core: 2. Of those that a mesh axis runs over, the one named last changes fastest.
Arguments:
- trajectory: float32 [32, 4, 64, 64, 128], P('tm', None, 'space'), may hold values from -6 to 6
- noise: bfloat16 [32, 4, 64, 64, 128], P('tm', None, 'space'), may hold values from -6 to 6
- timesteps: int32 [33], replicated, may hold values from 0 to 1000, as said below
- w_in: bfloat16 [128, 108], replicated, may hold values from -0.625 to 0.625
- w_time: bfloat16 [128, 128], replicated, may hold values from -0.5 to 0.5
- w_out: bfloat16 [4, 128], replicated, may hold values from -0.5 to 0.5
- well_cells: int32 [8192], P('space'), may hold values from 0 to 65535
- well_owner: int32 [8192, 1], P('space'), may hold values from 0 to 7; in each aligned block of 1024 rows (0 to 1023, 1024 to 2047, ...) at most 512 rows name the same one
- well_values: float32 [8192, 4], P('space'), may hold values from -6 to 6
Outputs:
- states: float32 [32, 4, 64, 64, 128], P('tm', None, 'space')
Inputs may be any that keep to these rules, and one draw needn't show every extreme that they name: `timesteps`: strictly falling; the first entry is 1000 and the last 0. `well_cells`: cells are numbered depth first, then the first and the second lateral dimension, within the owning slab. `well_owner`: among the rows of one index of space at most 512 name the same slab, and on some index exactly 512 do.
All inputs are finite; a program needn't handle non-finite values.
Results may differ from a plain program's by a relative error of at most 0.0011.
Values may be sent and summed in bfloat16 or wider, within the bound.
No kernel may reach another device: no remote copies, remote signals or barrier semaphores. Data moves between devices by JAX's collectives and lax.ppermute only.
A program may use at most 192 MiB of HBM per device.

v0:
```python
import math

import jax
import jax.numpy as jnp
from jax import lax
from jax.sharding import PartitionSpec as P

SWEEPS = 2


GUIDE_GAIN = 2.0
NOISE_COEF = 0.5
TIME_SCALE = 500.0


def with_halo(block, sides, width):
    for axis, dim in sides:
        count = lax.axis_size(axis)
        forward = [(i, i + 1) for i in range(count - 1)]
        backward = [(target, source) for source, target in forward]
        low = lax.ppermute(
            lax.slice_in_dim(block, block.shape[dim] - width, None, axis=dim), axis, forward
        )
        high = lax.ppermute(lax.slice_in_dim(block, 0, width, axis=dim), axis, backward)
        block = jnp.concatenate([low, block, high], axis=dim)
    return block


def entering(value, axis, join, neutral):
    count, mine = (lax.axis_size(axis), lax.axis_index(axis))
    pieces = lax.all_gather(value, axis)
    so_far = jnp.full_like(value, 0) + jnp.asarray(neutral, value.dtype)

    def turn(position, so_far):
        longer = join(so_far, pieces[position])
        return jnp.where(position < mine, longer, so_far)

    return lax.fori_loop(0, count - 1, turn, so_far)


def conv_drift(padded, w_in, time_bias, w_out):
    channels = padded.shape[0]
    depth_count = padded.shape[1] - 2
    first_len = padded.shape[2]
    second_len = padded.shape[3]
    hidden_width = w_in.shape[0]
    kernel = jnp.transpose(w_in.reshape(hidden_width, 3, 3, 3, channels), (0, 4, 1, 2, 3))
    numbers = ("NCDHW", "OIDHW", "NCDHW")

    def one_layer(depth_index, result):
        slices = lax.dynamic_slice_in_dim(padded, depth_index, 3, 1)
        before = lax.conv_general_dilated(
            slices[None],
            kernel,
            (1, 1, 1),
            [(0, 0), (1, 1), (1, 1)],
            dimension_numbers=numbers,
            preferred_element_type=jnp.float32,
        )
        before = before.reshape(hidden_width, first_len * second_len) + time_bias[:, None]
        hidden = jax.nn.silu(before).astype(jnp.bfloat16)
        layer = jnp.dot(w_out, hidden, preferred_element_type=jnp.float32)
        layer = layer.reshape(channels, 1, first_len, second_len)
        return lax.dynamic_update_slice_in_dim(result, layer, depth_index, 1)

    result = jnp.zeros((channels, depth_count, first_len, second_len), jnp.float32)
    return lax.fori_loop(0, depth_count, one_layer, result)


def time_embed(w_time, time_now):
    half_width = w_time.shape[1] // 2
    frequency = jnp.exp(-math.log(10000.0) * jnp.arange(half_width, dtype=jnp.float32) / half_width)
    angles = time_now.astype(jnp.float32) * frequency
    features = jnp.concatenate([jnp.sin(angles), jnp.cos(angles)]).astype(jnp.bfloat16)
    return jnp.dot(w_time, features, preferred_element_type=jnp.float32)


def increment(
    state, padded, noise_step, time_now, time_next, w_in, w_time, w_out, observed, well_count
):
    step_size = (time_now - time_next).astype(jnp.float32) / TIME_SCALE
    drift = conv_drift(padded, w_in, time_embed(w_time, time_now), w_out)
    drift = drift + GUIDE_GAIN * (observed - well_count * state)
    return step_size * drift + jnp.sqrt(step_size) * NOISE_COEF * noise_step.astype(jnp.float32)


def add_pair(earlier_part, later_part):
    return earlier_part + later_part


def per_device(
    trajectory, noise, timesteps, w_in, w_time, w_out, well_cells, well_owner, well_values
):
    step_count = trajectory.shape[0]
    channels = trajectory.shape[1]
    depth_count = trajectory.shape[2]
    first_len = trajectory.shape[3]
    second_len = trajectory.shape[4]
    slab_cells = depth_count * first_len * second_len
    time_rank = lax.axis_index("tm")
    is_first = time_rank == 0
    slab_count = lax.axis_size("space")
    capacity = well_cells.shape[0] // 2
    owners = well_owner[:, 0]
    onehot = (owners[:, None] == jnp.arange(slab_count, dtype=jnp.int32)[None, :]).astype(jnp.int32)
    slot_rank = jnp.sum(onehot * (jnp.cumsum(onehot, axis=0) - 1), axis=1)
    slot_index = owners * capacity + slot_rank
    send_values = (
        jnp.zeros((slab_count * capacity, channels), jnp.float32).at[slot_index].set(well_values)
    )
    send_cells = (
        jnp.full((slab_count * capacity,), -1.0, jnp.float32)
        .at[slot_index]
        .set(well_cells.astype(jnp.float32))
    )
    got_values, got_cells = (
        lax.all_to_all(
            send_values.reshape(slab_count, capacity, channels),
            "space",
            split_axis=0,
            concat_axis=0,
            tiled=True,
        ),
        lax.all_to_all(
            send_cells.reshape(slab_count, capacity),
            "space",
            split_axis=0,
            concat_axis=0,
            tiled=True,
        ),
    )
    row_values = got_values.reshape(-1, channels)
    row_cells = got_cells.reshape(-1)
    is_valid = row_cells >= 0.0
    target = jnp.where(is_valid, row_cells.astype(jnp.int32), slab_cells)
    observed = (
        jnp.zeros((slab_cells + 1, channels), jnp.float32).at[target].add(row_values)[:slab_cells]
    )
    observed = jnp.transpose(
        observed.reshape(depth_count, first_len, second_len, channels), (3, 0, 1, 2)
    )
    well_count = (
        jnp.zeros((slab_cells + 1,), jnp.float32).at[target].add(is_valid.astype(jnp.float32))
    )
    well_count = well_count[:slab_cells].reshape(depth_count, first_len, second_len)
    local_times = lax.dynamic_slice_in_dim(timesteps, time_rank * step_count, step_count + 1)
    start_keep = jnp.where(is_first, trajectory[0], 0.0)
    states = [trajectory[local_step] for local_step in range(step_count)]
    finished = states
    for sweep_index in range(SWEEPS):
        increments = []
        for local_step in range(step_count):
            state = states[local_step]
            padded = with_halo(state.astype(jnp.bfloat16), (("space", 1),), 1)
            increments.append(
                increment(
                    state,
                    padded,
                    noise[local_step],
                    local_times[local_step],
                    local_times[local_step + 1],
                    w_in,
                    w_time,
                    w_out,
                    observed,
                    well_count,
                )
            )
        own_terms = [increments[0] + start_keep] + increments[1:]
        running = own_terms[0]
        inclusive = [running]
        local_step = 1
        running = running + own_terms[local_step]
        inclusive.append(running)
        earlier = entering(running, "tm", add_pair, jnp.zeros_like(running))
        finished = [earlier + partial_sum for partial_sum in inclusive]
        next_first = earlier + start_keep
        states = [next_first] + finished[:-1]
    return jnp.stack(finished)


def solution(mesh):
    return jax.shard_map(
        per_device,
        mesh=mesh,
        in_specs=(
            P("tm", None, "space", None, None),
            P("tm", None, "space", None, None),
            P(),
            P(),
            P(),
            P(),
            P("space"),
            P("space", None),
            P("space", None),
        ),
        out_specs=P("tm", None, "space", None, None),
        check_vma=False,
    )
```

profile of v0, /device:TPU:0, one launch (start us, length us, event | category | flops | bytes accessed | tf_op | source)
XLA Modules:
  0.0 1238.2 jit_solution(4001615739779243436)
XLA Ops:
  11.6 5.9 collective-permute-start
  29.2 6.8 all-to-all-start
  53.8 28.0 %scatter_custom_fusion.3 = f32[65537]{0:T(1024)S(1)} fusion(s32[4096]{0:T(1024)S(1)} %bitcast.389, f32[4096]{0:T(1024)S(1)} %bitcast.391, f32[]{:T(128)} %constant.215.clone.1), kind=kCustom, calls=%fused_computation.121 | custom fusion | flops 4096 | bytes 262152 | tf_op jit(solution)/shard_map/scatter-add | solution.py:143
  83.2 53.8 %scatter_custom_fusion.2 = f32[65537,4]{1,0:T(8,128)} fusion(s32[4096]{0:T(1024)S(1)} %bitcast.390, f32[4096,4]{1,0:T(8,128)S(1)} %copy.165, f32[]{:T(128)} %constant.215.clone.1), kind=kCustom, calls=%fused_computation.74 | custom fusion | flops 16384 | bytes 1048596 | tf_op jit(solution)/shard_map/scatter-add | solution.py:137
  136.9 22.3 %slice.103 = f32[65536,4]{1,0:T(8,128)} slice(f32[65537,4]{1,0:T(8,128)} %scatter_custom_fusion.2), slice={[0:65536], [0:4]} | slice | bytes 2097152 | tf_op jit(solution)/shard_map/slice | solution.py:137
  159.2 20.3 %copy.166 = f32[8,64,128,4]{2,1,0,3:T(8,128)} copy(f32[8,64,128,4]{3,2,1,0:T(8,128)} %bitcast.367) | data formatting | bytes 2097152 | tf_op jit(solution)/shard_map/reshape | solution.py:140
  180.7 185.5 %while.81 = (s32[]{:T(128)}, f32[4,8,64,128]{3,2,1,0:T(8,128)}, bf16[4,10,64,128]{3,2,1,0:T(8,128)(2,1)S(1)}, bf16[128,4,3,3,3]{0,1,4,3,2:T(4,128)(2,1)S(1)}, f3...) while((s32[]{:T(128)}, f32[4,8,64,128]{3,2,1,0:T(8,128)}, ...), condition=%wide.region_10.11_spmd, body=%wide.region_9.10_spmd.sunk | while | flops 254636032 | bytes 46084384 | solution.py:67
  187.7 9.8 broadcast_select_fusion.9
  210.9 9.8 broadcast_select_fusion.9
  228.3 5.5 copy.226
  234.1 9.8 broadcast_select_fusion.9
  257.3 9.8 broadcast_select_fusion.9
  280.5 9.8 broadcast_select_fusion.9
  303.7 9.8 broadcast_select_fusion.9
  326.9 9.8 broadcast_select_fusion.9
  350.0 9.8 broadcast_select_fusion.9
  368.5 185.8 %while.80 = (s32[]{:T(128)}, f32[4,8,64,128]{3,2,1,0:T(8,128)}, bf16[4,10,64,128]{3,2,1,0:T(8,128)(2,1)S(1)}, bf16[128,4,3,3,3]{0,1,4,3,2:T(4,128)(2,1)S(1)}, f3...) while((s32[]{:T(128)}, f32[4,8,64,128]{3,2,1,0:T(8,128)}, ...), condition=%wide.region_1.2_spmd, body=%wide.region_0.0_spmd.sunk | while | flops 254636032 | bytes 46084384 | solution.py:67
  370.2 5.5 copy.221
  375.9 9.8 broadcast_select_fusion.8
  399.1 9.8 broadcast_select_fusion.8
  422.3 9.8 broadcast_select_fusion.8
  445.4 9.8 broadcast_select_fusion.8
  468.6 9.8 broadcast_select_fusion.8
  491.8 9.8 broadcast_select_fusion.8
  515.0 9.8 broadcast_select_fusion.8
  538.1 9.8 broadcast_select_fusion.8
  559.5 113.2 %all-gather.5.cloned.1.call-done = f32[64,8,64,128]{3,2,1,0:T(8,128)} async-done(((f32[4,8,64,128]{3,2,1,0:T(8,128)}), f32[64,8,64,128]{3,2,1,0:T(8,128)}) %all-gather.5.cloned.1.call-update) | async-done | bytes 16777232 | tf_op jit(solution)/shard_map/all_gather | solution.py:31
  672.7 24.4 %while.84 = (s32[]{:T(128)}, f32[4,8,64,128]{3,2,1,0:T(8,128)S(1)}, s32[]{:T(128)}, f32[16,4,8,64,128]{4,3,2,1,0:T(8,128)}, s32[]{:T(128)}, /*index=5*/s32[]{:T(128)}) while((s32[]{:T(128)}, f32[4,8,64,128]{3,2,1,0:T(8,128)S(1)}, s32[]{:T(128)}, f32[16,4,8,64,128]{4,3,2,1,0:T(8,128)}, s32[]{:T(128)}, ...), condition=%wide.region_12.13_spmd.clone, body=%wide.region_11.12_spmd.clone.sunk | while | flops 786436 | bytes 3145821 | solution.py:38
  709.6 185.7 %while.82 = (s32[]{:T(128)}, f32[4,8,64,128]{3,2,1,0:T(8,128)}, bf16[4,10,64,128]{3,2,1,0:T(8,128)(2,1)S(1)}, bf16[128,4,3,3,3]{0,1,4,3,2:T(4,128)(2,1)S(1)}, f3...) while((s32[]{:T(128)}, f32[4,8,64,128]{3,2,1,0:T(8,128)}, ...), condition=%wide.region_14.15_spmd, body=%wide.region_13.14_spmd.sunk | while | flops 254636032 | bytes 46084384 | solution.py:67
  716.8 9.8 broadcast_select_fusion.10
  740.0 9.8 broadcast_select_fusion.10
  763.2 9.8 broadcast_select_fusion.10
  786.4 9.8 broadcast_select_fusion.10
  809.6 9.8 broadcast_select_fusion.10
  832.8 9.8 broadcast_select_fusion.10
  856.0 9.8 broadcast_select_fusion.10
  879.2 9.8 broadcast_select_fusion.10
  897.6 185.9 %while.83 = (s32[]{:T(128)}, f32[4,8,64,128]{3,2,1,0:T(8,128)}, bf16[4,10,64,128]{3,2,1,0:T(8,128)(2,1)S(1)}, bf16[128,4,3,3,3]{0,1,4,3,2:T(4,128)(2,1)S(1)}, f3...) while((s32[]{:T(128)}, f32[4,8,64,128]{3,2,1,0:T(8,128)}, ...), condition=%wide.region_16.17_spmd, body=%wide.region_15.16_spmd.sunk | while | flops 254636032 | bytes 46084384 | solution.py:67
  904.8 9.8 broadcast_select_fusion.11
  928.0 9.8 broadcast_select_fusion.11
  951.2 9.8 broadcast_select_fusion.11
  974.4 9.8 broadcast_select_fusion.11
  997.5 9.8 broadcast_select_fusion.11
  1020.7 9.8 broadcast_select_fusion.11
  1043.9 9.8 broadcast_select_fusion.11
  1067.1 9.8 broadcast_select_fusion.11
  1088.7 113.5 %all-gather.7.cloned.1.call-done = f32[64,8,64,128]{3,2,1,0:T(8,128)} async-done(((f32[4,8,64,128]{3,2,1,0:T(8,128)}), f32[64,8,64,128]{3,2,1,0:T(8,128)}) %all-gather.7.cloned.1.call-update) | async-done | bytes 16777232 | tf_op jit(solution)/shard_map/all_gather | solution.py:31
  1202.1 24.4 %while.85 = (s32[]{:T(128)}, f32[4,8,64,128]{3,2,1,0:T(8,128)S(1)}, s32[]{:T(128)}, f32[16,4,8,64,128]{4,3,2,1,0:T(8,128)}, s32[]{:T(128)}, /*index=5*/s32[]{:T(128)}) while((s32[]{:T(128)}, f32[4,8,64,128]{3,2,1,0:T(8,128)S(1)}, s32[]{:T(128)}, f32[16,4,8,64,128]{4,3,2,1,0:T(8,128)}, s32[]{:T(128)}, ...), condition=%wide.region_18.19_spmd.clone, body=%wide.region_17.18_spmd.clone.sunk | while | flops 786436 | bytes 3145821 | solution.py:38
  (602 shorter events, 526.6 us)
Async XLA Ops:
  6.5 32.2 %copy-start = (bf16[128,128]{1,0:T(8,128)(2,1)S(1)}, bf16[128,128]{1,0:T(8,128)(2,1)}, u32[]{:S(2)}) copy-start(bf16[128,128]{1,0:T(8,128)(2,1)} %param.25) | copy-start | bytes 98308
  8.3 2.6 copy-start.16
  8.3 171.2 %collective-permute-start.2 = (bf16[4,1,64,128]{3,2,1,0:T(8,128)(2,1)S(1)}, bf16[4,1,64,128]{3,2,1,0:T(8,128)(2,1)S(1)}, u32[]{:S(2)}, u32[]{:S(2)}) collective-permute-start(bf16[4,1,64,128]{3,2,1,0:T(8,128)(2,1)S(1)} %get-tuple-element.857), channel_id=1, source_target_pairs={{0,1},{1,2},{2,3},{3,4},{4,5},{5,6},{6,7},{8,9},{9,10},{10,11},{11... | collective-permute-start | bytes 196616 | tf_op jit(solution)/shard_map/ppermute | solution.py:21
  9.6 169.9 %collective-permute-start.3 = (bf16[4,1,64,128]{3,2,1,0:T(8,128)(2,1)S(1)}, bf16[4,1,64,128]{3,2,1,0:T(8,128)(2,1)S(1)}, u32[]{:S(2)}, u32[]{:S(2)}) collective-permute-start(bf16[4,1,64,128]{3,2,1,0:T(8,128)(2,1)S(1)} %get-tuple-element.858), channel_id=1, source_target_pairs={{1,0},{2,1},{3,2},{4,3},{5,4},{6,5},{7,6},{9,8},{10,9},{11,10},{12... | collective-permute-start | bytes 196616 | tf_op jit(solution)/shard_map/ppermute | solution.py:24
  11.6 354.6 %collective-permute-start = (bf16[4,1,64,128]{3,2,1,0:T(8,128)(2,1)}, bf16[4,1,64,128]{3,2,1,0:T(8,128)(2,1)}, u32[]{:S(2)}, u32[]{:S(2)}) collective-permute-start(bf16[4,1,64,128]{3,2,1,0:T(8,128)(2,1)} %get-tuple-element.855), channel_id=1, source_target_pairs={{0,1},{1,2},{2,3},{3,4},{4,5},{5,6},{6,7},{8,9},{9,10},{10,11},{11... | collective-permute-start | bytes 196616 | tf_op jit(solution)/shard_map/ppermute | solution.py:21
  17.5 348.8 %collective-permute-start.1 = (bf16[4,1,64,128]{3,2,1,0:T(8,128)(2,1)}, bf16[4,1,64,128]{3,2,1,0:T(8,128)(2,1)}, u32[]{:S(2)}, u32[]{:S(2)}) collective-permute-start(bf16[4,1,64,128]{3,2,1,0:T(8,128)(2,1)} %get-tuple-element.856), channel_id=1, source_target_pairs={{1,0},{2,1},{3,2},{4,3},{5,4},{6,5},{7,6},{9,8},{10,9},{11,10},{12... | collective-permute-start | bytes 196616 | tf_op jit(solution)/shard_map/ppermute | solution.py:24
  29.2 19.6 %all-to-all-start = ((f32[8,1,512]{2,1,0:T(1,128)}), f32[8,1,512]{2,1,0:T(1,128)S(1)}, u32[]{:S(2)}, u32[]{:S(2)}) async-start(f32[8,1,512]{2,1,0:T(1,128)} %bitcast.39), calls=%async_computation | async-start | bytes 32768 | tf_op jit(solution)/shard_map/all_to_all | solution.py:124
  48.8 33.7 %all-to-all-start.1 = ((f32[8,512,4]{1,2,0:T(4,128)}), f32[8,512,4]{1,2,0:T(4,128)S(1)}, u32[]{:S(2)}, u32[]{:S(2)}) async-start(f32[8,512,4]{1,2,0:T(4,128)} %copy.164), calls=%async_computation.1 | async-start | bytes 131072 | tf_op jit(solution)/shard_map/all_to_all | solution.py:117
  53.6 619.0 %all-gather.5.cloned.1.call-start = ((), (), s32[]{:S(2)}) async-start(), calls=%async_computation.2 | async-start | bytes 17825792 | tf_op jit(solution)/shard_map/all_gather | solution.py:31
  159.2 21.5 %copy-start.17 = (bf16[4,128]{1,0:T(4,128)(2,1)S(1)}, bf16[4,128]{1,0:T(4,128)(2,1)}, u32[]{:S(2)}) copy-start(bf16[4,128]{1,0:T(4,128)(2,1)} %param.26) | copy-start | bytes 3076
  159.2 21.5 %copy-start.21 = (pred[8,17]{0,1:T(8,128)(4,1)S(1)}, pred[8,17]{0,1:T(8,128)(4,1)}, u32[]{:S(2)}) copy-start(pred[8,17]{0,1:T(8,128)(4,1)} %constant.422) | copy-start | bytes 412
  180.7 187.8 %copy-start.20 = (f32[128]{0:T(128)S(1)}, f32[128]{0:T(128)}, u32[]{:S(2)}) copy-start(f32[128]{0:T(128)} %convolution_bitcast_fusion.5) | copy-start | bytes 1540
  201.5 2.4 copy-start.12
  224.6 2.4 copy-start.12
  247.8 2.4 copy-start.12
  271.0 2.4 copy-start.12
  294.2 2.4 copy-start.12
  317.4 2.4 copy-start.12
  340.6 2.4 copy-start.12
  363.8 2.4 copy-start.12
  459.2 2.4 copy-start.14
  505.5 2.4 copy-start.14
  559.4 642.7 %all-gather.7.cloned.1.call-start = ((), (), s32[]{:S(2)}) async-start(), calls=%async_computation.3 | async-start | bytes 17825792 | tf_op jit(solution)/shard_map/all_gather | solution.py:31
  672.7 24.4 %copy-start.4 = (f32[2,4,8,64,128]{4,3,2,1,0:T(8,128)S(1)}, f32[2,4,8,64,128]{4,3,2,1,0:T(8,128)}, u32[]{:S(2)}) copy-start(f32[2,4,8,64,128]{4,3,2,1,0:T(8,128)} %param.21) | copy-start | bytes 6291460
  697.0 12.6 %copy-start.2 = (f32[4,8,64,128]{3,2,1,0:T(8,128)}, f32[4,8,64,128]{3,2,1,0:T(8,128)S(1)}, u32[]{:S(2)}) copy-start(f32[4,8,64,128]{3,2,1,0:T(8,128)S(1)} %get-tuple-element.601) | copy-start | bytes 3145732
  699.0 9.4 copy-start.15
  699.0 9.4 collective-permute-start.4
  700.8 7.7 collective-permute-start.5
  702.7 192.6 %collective-permute-start.6 = (bf16[4,1,64,128]{3,2,1,0:T(8,128)(2,1)}, bf16[4,1,64,128]{3,2,1,0:T(8,128)(2,1)S(1)}, u32[]{:S(2)}, u32[]{:S(2)}) collective-permute-start(bf16[4,1,64,128]{3,2,1,0:T(8,128)(2,1)} %get-tuple-element.853), channel_id=1, source_target_pairs={{0,1},{1,2},{2,3},{3,4},{4,5},{5,6},{6,7},{8,9},{9,10},{10,11},{11... | collective-permute-start | bytes 196616 | tf_op jit(solution)/shard_map/ppermute | solution.py:21
  707.1 188.2 %collective-permute-start.7 = (bf16[4,1,64,128]{3,2,1,0:T(8,128)(2,1)}, bf16[4,1,64,128]{3,2,1,0:T(8,128)(2,1)S(1)}, u32[]{:S(2)}, u32[]{:S(2)}) collective-permute-start(bf16[4,1,64,128]{3,2,1,0:T(8,128)(2,1)} %get-tuple-element.854), channel_id=1, source_target_pairs={{1,0},{2,1},{3,2},{4,3},{5,4},{6,5},{7,6},{9,8},{10,9},{11,10},{12... | collective-permute-start | bytes 196616 | tf_op jit(solution)/shard_map/ppermute | solution.py:24
  709.6 187.9 %copy-start.19 = (f32[128]{0:T(128)S(1)}, f32[128]{0:T(128)}, u32[]{:S(2)}) copy-start(f32[128]{0:T(128)} %copy-done.18) | copy-start | bytes 1540
  730.6 2.4 copy-start.10
  753.8 2.4 copy-start.10
  777.0 2.4 copy-start.10
  846.5 2.4 copy-start.10
  869.7 2.4 copy-start.10
  918.5 2.4 copy-start.8
  941.7 2.4 copy-start.8
  964.9 2.4 copy-start.8
  988.1 2.4 copy-start.8
  1011.3 2.4 copy-start.8
  1034.5 2.4 copy-start.8
  1057.7 2.4 copy-start.8
  1080.8 2.4 copy-start.8
  1202.1 24.4 %copy-start.3 = (f32[4,8,64,128]{3,2,1,0:T(8,128)S(1)}, f32[4,8,64,128]{3,2,1,0:T(8,128)}, u32[]{:S(2)}) copy-start(f32[4,8,64,128]{3,2,1,0:T(8,128)} %copy-done.2) | copy-start | bytes 3145732
  1202.1 24.4 %copy-start.5 = (f32[8,64,128,4]{2,1,0,3:T(8,128)S(1)}, f32[8,64,128,4]{2,1,0,3:T(8,128)}, u32[]{:S(2)}) copy-start(f32[8,64,128,4]{2,1,0,3:T(8,128)} %copy.166) | copy-start | bytes 3145732
  1202.1 24.4 %copy-start.6 = (f32[65536]{0:T(1024)S(1)}, f32[65536]{0:T(1024)}, u32[]{:S(2)}) copy-start(f32[65536]{0:T(1024)} %slice.104) | copy-start | bytes 786436
  1226.5 4.4 copy-start.1
  (42 other events, 64.5 us)
Sparse Core Ops, SparseCore 0:
  559.6 113.0 all-gather.4
  1088.8 113.3 all-gather.6
where the time goes:
time: 1250 us; the launch traced here: 1240 us
  local copies, waits for them, and re-layouts  434 us (35%)
  matrix products  336 us (27%)
  waiting for transfers between devices  227 us (18%)
  other arithmetic  189 us (15%)
  starting transfers between devices  30.1 us (2%)
  between operations  18.2 us (1%)
    conv_general_dilated x32, matrix products, one_layer(): lax.conv_general_dilated(slices[None], kernel, (1, 1, 1), [(0, 0), (1, 1)...  315 us
    conv_general_dilated x160, local copies, waits for them, and re-layouts, one_layer(): lax.conv_general_dilated(slices[None], kernel, (1, 1, 1), [(0, 0), (1, 1)...  308 us
    all_gather x2, waiting for transfers between devices, entering(): pieces = lax.all_gather(value, axis)  227 us
    scatter-add x1, other arithmetic, per_device(): jnp.zeros((slab_cells + 1, channels), jnp.float32).at[target]  53.8 us
    select_n x30, other arithmetic, turn(): return jnp.where(position < mine, longer, so_far)  48 us
    convert_element_type x32, other arithmetic, one_layer(): hidden = jax.nn.silu(before).astype(jnp.bfloat16)  35 us
    broadcast_in_dim x32, local copies, waits for them, and re-layouts, one_layer(): slices[None]  31.3 us
    scatter-add x1, other arithmetic, per_device(): jnp.zeros((slab_cells + 1,), jnp.float32).at[target]  28 us
  transfers between devices with their start and end apart: 12, of which 2 were waited for; matrix products, arithmetic and copies ran while one was open for 42% of the time, Pallas kernels for 0%

commit v1 on v0

v1 whole, which is shorter than its diff:
```python
import functools
import math

import jax
import jax.numpy as jnp
import numpy as np
from jax import lax
from jax.experimental import pallas as pl
from jax.experimental.pallas import tpu as pltpu
from jax.sharding import PartitionSpec as P

F32, BF16, I16 = jnp.float32, jnp.bfloat16, jnp.int16
C, HID, ND, NX, NY = 4, 128, 8, 64, 128
TM, SPACE = 16, 8
ROWS = 1024
GUIDE_GAIN = 2.0
NOISE_COEF = 0.5
TIME_SCALE = 500.0
EXP = 16
PAY = 2 * NX + EXP
GPAY = 5 * 32 + EXP
MIB = 2**20


def params(mib):
    return pltpu.CompilerParams(vmem_limit_bytes=mib * MIB)


def smem():
    return pl.BlockSpec(memory_space=pltpu.SMEM)


def full(dims):
    return pl.BlockSpec(dims, lambda i: (0,) * len(dims), pipeline_mode=pl.Buffered(1))


def first_step(v):
    return pl.BlockSpec((1,) + v.shape[1:], lambda i: (0,) * v.ndim, pipeline_mode=pl.Buffered(1))


def call(kernel, name, mib, out_shape, scalars, *args, scratch=(), first=()):
    return pl.pallas_call(
        kernel,
        grid=(1,),
        in_specs=[smem()] * len(scalars) + [first_step(v) if i in first else full(v.shape) for i, v in enumerate(args)],
        out_specs=jax.tree.map(lambda v: full(v.shape), out_shape),
        out_shape=out_shape,
        scratch_shapes=list(scratch),
        compiler_params=params(mib),
        name=name,
    )(*scalars, *args)


def shape(dtype, *dims):
    return jax.ShapeDtypeStruct(dims, dtype)


def selection():
    sel = np.zeros((4, 108, 256), np.float32)
    for xx in range(2):
        for dd in range(2):
            for a in range(3):
                for b in range(3):
                    for e in range(3):
                        for c in range(C):
                            sel[xx * 2 + dd, (9 * a + 3 * b + e) * C + c, (xx + b) * 48 + e * 16 + (dd + a) * 4 + c] = 0.5
    return sel


def pack_kernel(owner_hbm, cell_hbm, value_hbm, traj_hbm, rows_ref, top_ref, bottom_ref, owner, cell, value, first, last, sems):
    copies = [
        pltpu.make_async_copy(src, dst, sems.at[i])
        for i, (src, dst) in enumerate([
            (owner_hbm, owner), (cell_hbm, cell), (value_hbm, value),
            (traj_hbm.at[:, :, 0], first), (traj_hbm.at[:, :, ND - 1], last),
        ])
    ]
    for copy in copies:
        copy.start()
    for copy in copies:
        copy.wait()
    rows = jnp.concatenate(
        [owner[...].astype(F32), cell[...].astype(F32), value[...], jnp.zeros((2, ROWS), F32)], 0
    )
    for k in range(SPACE):
        rows_ref[k] = rows
    top_ref[...] = first[...].astype(BF16)
    bottom_ref[...] = last[...].astype(BF16)


def pack(owner, cells, values, trajectory):
    edge = shape(BF16, 2, C, NX, NY)
    out_shape = [shape(F32, SPACE, 8, ROWS), edge, edge]
    layer = pltpu.VMEM((2, C, NX, NY), F32)
    return pl.pallas_call(
        pack_kernel,
        grid=(1,),
        in_specs=[pl.BlockSpec(memory_space=pltpu.HBM)] * 4,
        out_specs=[full(v.shape) for v in out_shape],
        out_shape=out_shape,
        scratch_shapes=[
            pltpu.VMEM((1, ROWS), jnp.int32), pltpu.VMEM((1, ROWS), jnp.int32), pltpu.VMEM((C, ROWS), F32),
            layer, layer, pltpu.SemaphoreType.DMA((5,)),
        ],
        compiler_params=params(8),
        name="pack",
    )(owner, cells, values, trajectory)


def weights_kernel(rank_ref, w_ref, sel_ref, bias_ref, out_ref, wbig_ref, w2_ref):
    lane = lax.broadcasted_iota(jnp.int32, (HID, 256), 1)
    all_steps = bias_ref[...]
    column = lax.broadcasted_iota(jnp.int32, all_steps.shape, 1)
    extra = []
    for j in range(2):
        b = jnp.sum(jnp.where(column == 2 * rank_ref[0] + j, all_steps, 0.0), axis=1, keepdims=True) * 0.5
        b1 = b.astype(BF16).astype(F32)
        b2 = (b - b1).astype(BF16).astype(F32)
        b3 = b - b1 - b2
        extra.append(jnp.where(lane == 192, b1, jnp.where(lane == 193, b2, jnp.where(lane == 194, b3, 0.0))))
    for k in range(4):
        wk = lax.dot_general(w_ref[...], sel_ref[k], (((0,), (0,)), ((), ())), preferred_element_type=F32)
        for j in range(2):
            wbig_ref[j, k * HID:(k + 1) * HID, :] = (wk + extra[j]).astype(BF16)
    pick = lax.broadcasted_iota(jnp.int32, (16, C), 0) % C == lax.broadcasted_iota(jnp.int32, (16, C), 1)
    tall = jnp.dot(jnp.where(pick, 1.0, 0.0).astype(BF16), out_ref[...], preferred_element_type=F32)
    wide = jnp.concatenate([tall] * 4, 1)
    own = lax.broadcasted_iota(jnp.int32, (16, 512), 0) // C == lax.broadcasted_iota(jnp.int32, (16, 512), 1) // HID
    w2_ref[...] = jnp.where(own, wide, 0.0).astype(BF16)


INNER, OUTER = (1, 2), (0, 3)
CONV_SCRATCH = [
    pltpu.VMEM((NX * 40, NY), F32),
    pltpu.VMEM((2, 66 * 48, NY), BF16),
    pltpu.VMEM((72 * 16, NY), F32),
    pltpu.VMEM((4, 512, 256), BF16),
    pltpu.VMEM((4, 512, 256), BF16),
]


def clear(Q, HB):
    zt = jnp.zeros((48, NY), BF16)
    for i in range(2):
        Q[i, 0:48, :] = zt
        Q[i, 65 * 48:66 * 48, :] = zt
    HB[...] = jnp.zeros(HB.shape, BF16)


def conv_step(layer, pairs, wbig, w2_ref, put, S, Q, So, HA, HB):
    for dp in sorted({2 * p + i for p in pairs for i in range(4)}):
        for c in range(C):
            S[pl.ds(dp * 4 + c, NX, stride=40), :] = layer(c, dp)
    lane = lax.broadcasted_iota(jnp.int32, (16, NY), 1)

    def prep(x, carry):
        base = pl.multiple_of((x + 1) * 48, 16)
        for i, p in enumerate(pairs):
            v = S[pl.ds(pl.multiple_of(x * 40 + 8 * p, 8), 16), :]
            ve = [
                jnp.where(lane == 0, 0.0, pltpu.roll(v, 1, 1)),
                v,
                jnp.where(lane == NY - 1, 0.0, pltpu.roll(v, NY - 1, 1)),
            ]
            for e in range(3):
                Q[i, pl.ds(base + 16 * e, 16), :] = ve[e].astype(BF16)
        return carry

    lax.fori_loop(0, NX, prep, 0, unroll=8)
    ones = jnp.ones((16, 256), BF16)

    def first(t, hidden):
        for g in range(4):
            xq, i = 2 * t + g // 2, g % 2
            b0 = pl.multiple_of(xq * 192, 16)
            pa = Q[i, pl.ds(b0, 192), :]
            pb = Q[i, pl.ds(b0 + 96, 192), :]
            patch = jnp.concatenate([jnp.concatenate([pa, pb], 1), ones], 0)
            u = jnp.dot(wbig[:, 0:208], patch, preferred_element_type=F32)
            hidden[g] = (u + u * jnp.tanh(u)).astype(BF16)
            yield

    def second(t, hidden):
        for g in range(4):
            xq, i = 2 * t + g // 2, g % 2
            r = jnp.dot(w2_ref[...], hidden[g], preferred_element_type=F32)
            for hh in range(2):
                for xx in range(2):
                    st = pl.multiple_of((xq * 4 + 8 + 2 * hh + xx) * 16, 8)
                    So[pl.ds(st + i * 8, 8), :] = r[xx * 8:xx * 8 + 8, hh * NY:hh * NY + NY]
            yield

    def body(i, carry):
        for _ in zip(first(2 * i, HA), second(2 * i - 1, HB)):
            pass
        for _ in zip(first(2 * i + 1, HB), second(2 * i, HA)):
            pass
        return carry

    lax.fori_loop(0, NX // 16, body, 0)
    for _ in second(NX // 8 - 1, HB):
        pass
    for i in range(2):
        for dd in range(2):
            for c in range(C):
                put(c, 2 * i + dd, So[pl.ds(128 + i * 8 + dd * 4 + c, NX, stride=16), :])


def inner(state, wbig, w2_ref, o_ref, scratch):
    clear(scratch[1], scratch[4])
    for j in range(2):
        conv_step(
            lambda c, dp: state(j, c, dp - 1), INNER, wbig.at[j], w2_ref,
            lambda c, i, v: o_ref.__setitem__((j, c, i), v), *scratch,
        )


def outer(state, wbig, w2_ref, lo_ref, hi_ref, o_ref, scratch):
    clear(scratch[1], scratch[4])

    def layer(j, c, dp):
        if dp == 0:
            return lo_ref[j, c].astype(F32)
        if dp == ND + 1:
            return hi_ref[j, c].astype(F32)
        return state(j, c, dp - 1)

    for j in range(2):
        conv_step(
            lambda c, dp: layer(j, c, dp), OUTER, wbig.at[j], w2_ref,
            lambda c, i, v: o_ref.__setitem__((j, c, i), v), *scratch,
        )


def increments(state, rank_ref, ts_ref, in_ref, out_ref, n_ref, g_ref, start, pay_ref, sums_refs):
    tm = rank_ref[0]
    step, gain = [], []
    for j in range(2):
        span = jnp.full((1, NY), ts_ref[2 * tm + j] - ts_ref[2 * tm + j + 1], jnp.int32).astype(F32) / TIME_SCALE
        step.append(span)
        gain.append(jnp.sqrt(span) * NOISE_COEF)
    for p in range(4):
        for c in range(C):
            totals = []
            for dd in range(2):
                d = 2 * p + dd
                observed, count = guide_at(g_ref, d, c)
                total = start(c, d)
                for j in range(2):
                    drift = in_ref[j, c, d - 2] if p in INNER else out_ref[j, c, d if p == 0 else d - 4]
                    drift = drift + GUIDE_GAIN * (observed - count * state(j, c, d))
                    total = total + step[j] * drift + gain[j] * n_ref[j, c, d].astype(F32)
                    if j < len(sums_refs):
                        sums_refs[j][c, d] = total
                totals.append(total)
            encode(totals, lambda at, n, v: pay_ref.__setitem__((c, p, pl.ds(at, n), slice(None)), v))


def given(s_ref):
    return lambda j, c, d: s_ref[j, c, d]


def first_of(rank_ref, start_ref):
    keep = jnp.where(rank_ref[0] == 0, 1.0, 0.0)
    return lambda c, d: keep * start_ref[c, d]


def arrived(e_ref, start, sum_ref):
    def state(j, c, d):
        get = lambda at, n: e_ref[c, d // 2, pl.ds(at, n), :]
        entering = decode(get, d % 2, scale_of(get))
        return entering + (start(c, d) if j == 0 else sum_ref[c, d])

    return state


def inner1_kernel(s_ref, wbig, w2_ref, o_ref, *scratch):
    inner(given(s_ref), wbig, w2_ref, o_ref, scratch)


def inner2_kernel(rank_ref, e_ref, start_ref, sum_ref, wbig, w2_ref, o_ref, *scratch):
    inner(arrived(e_ref, first_of(rank_ref, start_ref.at[0]), sum_ref), wbig, w2_ref, o_ref, scratch)


def outer1_kernel(s_ref, wbig, w2_ref, lo_ref, hi_ref, o_ref, *scratch):
    outer(given(s_ref), wbig, w2_ref, lo_ref, hi_ref, o_ref, scratch)


def increments1_kernel(rank_ref, ts_ref, s_ref, in_ref, out_ref, n_ref, g_ref, pay_ref, sum_ref):
    start = first_of(rank_ref, s_ref.at[0])
    increments(given(s_ref), rank_ref, ts_ref, in_ref, out_ref, n_ref, g_ref, start, pay_ref, [sum_ref])


def outer2_kernel(
    rank_ref, ts_ref, e_ref, traj_ref, before_ref, wbig, w2_ref, lo_ref, hi_ref, in_ref, n_ref, g_ref,
    pay_ref, sum0_ref, sum1_ref, out_ref, *scratch,
):
    start = first_of(rank_ref, traj_ref.at[0])
    state = arrived(e_ref, start, before_ref)
    outer(state, wbig, w2_ref, lo_ref, hi_ref, out_ref, scratch)
    increments(state, rank_ref, ts_ref, in_ref, out_ref, n_ref, g_ref, start, pay_ref, [sum0_ref, sum1_ref])


def edges_kernel(rank_ref, e_ref, start_ref, sum_ref, top_ref, bottom_ref):
    state = arrived(e_ref, first_of(rank_ref, start_ref.at[0]), sum_ref)
    for j in range(2):
        for c in range(C):
            top_ref[j, c] = state(j, c, 0).astype(BF16)
            bottom_ref[j, c] = state(j, c, ND - 1).astype(BF16)


def last_kernel(e_ref, sum0_ref, sum1_ref, o_ref):
    for c in range(C):
        get = lambda at, n: e_ref[c, pl.ds(at, n), :]
        scale = scale_of(get)
        for dd in range(2):
            entering = decode(get, dd, scale)
            o_ref[0, c, dd] = entering + sum0_ref[c, dd]
            o_ref[1, c, dd] = entering + sum1_ref[c, dd]


def last_states(entering, sum0, sum1):
    one = lambda: pl.BlockSpec((C, 2, NX, NY), lambda p: (0, p, 0, 0))
    return pl.pallas_call(
        last_kernel,
        grid=(4,),
        in_specs=[pl.BlockSpec((C, None, PAY, NY), lambda p: (0, p, 0, 0)), one(), one()],
        out_specs=pl.BlockSpec((2, C, 2, NX, NY), lambda p: (0, 0, p, 0, 0)),
        out_shape=shape(F32, 2, C, ND, NX, NY),
        compiler_params=params(16),
        name="last_states",
    )(entering, sum0, sum1)


def wells_kernel(rank_ref, rows_ref, *refs):
    o_ref = refs[-1]
    me_tm, me_space = rank_ref[0], rank_ref[1]
    line = lax.broadcasted_iota(jnp.int32, (32, ROWS), 0) + 32 * me_tm
    column = lax.broadcasted_iota(jnp.int32, (NY, ROWS), 0)
    total = jnp.zeros((13 * 32, NY), F32)
    for src in range(SPACE):
        owner = rows_ref[src, 0:1, :].astype(jnp.int32)
        cell = rows_ref[src, 1:2, :].astype(jnp.int32)
        at_line = jnp.where(owner == me_space, cell >> 7, -1)
        hit = jnp.where(line == at_line, 1.0, 0.0)
        pieces = [hit]
        for c in range(C):
            v = rows_ref[src, 2 + c:3 + c, :]
            v1 = v.astype(BF16).astype(F32)
            v2 = (v - v1).astype(BF16).astype(F32)
            v3 = v - v1 - v2
            pieces += [hit * v1, hit * v2, hit * v3]
        left = jnp.concatenate(pieces, 0).astype(BF16)
        right = jnp.where(column == (cell & 127), 1.0, 0.0).astype(BF16)
        total = total + lax.dot_general(left, right, (((1,), (1,)), ((), ())), preferred_element_type=F32)
    observed = [total[at:at + 32] + total[at + 32:at + 64] + total[at + 64:at + 96] for at in range(32, 13 * 32, 96)]
    power, factor = power_of(observed)
    pieces = [jnp.round(v * factor) for v in observed] + [total[0:32], jnp.broadcast_to(power, (EXP, NY))]
    coded = jnp.concatenate(pieces, 0).astype(jnp.int32).astype(I16)
    for k in range(TM):
        o_ref[k] = coded


def wells(ranks, rows, *earlier):
    return pl.pallas_call(
        wells_kernel,
        grid=(1,),
        in_specs=[smem(), full(rows.shape)] + [pl.BlockSpec(memory_space=pl.ANY)] * len(earlier),
        out_specs=full((TM, GPAY, NY)),
        out_shape=shape(I16, TM, GPAY, NY),
        compiler_params=params(12),
        name="wells",
    )(ranks, rows, *earlier)


def guide_at(g_ref, d, c):
    observed, count = [], []
    for k in (2 * d, 2 * d + 1):
        wide = lambda at, n: g_ref[k, pl.ds(at, n), :].astype(jnp.int32).astype(F32)
        observed.append(wide(c * 32, 32) * jnp.exp2(wide(5 * 32, EXP)[0:1]))
        count.append(wide(4 * 32, 32))
    return jnp.concatenate(observed, 0), jnp.concatenate(count, 0)


def power_of(planes):
    top = functools.reduce(jnp.maximum, [jnp.max(jnp.abs(v), axis=0, keepdims=True) for v in planes])
    power = jnp.ceil(jnp.log2(jnp.maximum(top, 1e-30) * (1.0 / 32000.0)))
    return power, jnp.exp2(-power)


def encode(planes, put):
    power, factor = power_of(planes)
    for i in range(2):
        put(i * NX, NX, jnp.round(planes[i] * factor).astype(jnp.int32).astype(I16))
    put(2 * NX, EXP, jnp.broadcast_to(power, (EXP, NY)).astype(jnp.int32).astype(I16))


def scale_of(get):
    return jnp.exp2(get(2 * NX, EXP).astype(jnp.int32).astype(F32)[0:1])


def decode(get, i, scale):
    return get(i * NX, NX).astype(jnp.int32).astype(F32) * scale


def scan_kernel(got_ref, o_ref):
    running = [jnp.zeros((NX, NY), F32) for _ in range(2)]
    for k in range(TM):
        encode(running, lambda at, n, v: o_ref.__setitem__((k, pl.ds(at, n), slice(None)), v))
        if k < TM - 1:
            get = lambda at, n: got_ref[k, pl.ds(at, n), :]
            scale = scale_of(get)
            running = [running[i] + decode(get, i, scale) for i in range(2)]


def prefix(payload):
    got = lax.all_to_all(payload.reshape(TM, PAY, NY), "tm", 0, 0, tiled=True)
    ahead = call(scan_kernel, "scan", 6, shape(I16, TM, PAY, NY), [], got)
    return lax.all_to_all(ahead, "tm", 0, 0, tiled=True).reshape(C, 4, PAY, NY)


def halos(top, bottom):
    lo = lax.ppermute(bottom, "space", [(i, i + 1) for i in range(SPACE - 1)])
    hi = lax.ppermute(top, "space", [(i + 1, i) for i in range(SPACE - 1)])
    return lo, hi


def time_bias(w_time, times):
    half_width = w_time.shape[1] // 2
    frequency = jnp.exp(-math.log(10000.0) * jnp.arange(half_width, dtype=F32) / half_width)
    angles = times.astype(F32)[None, :] * frequency[:, None]
    features = jnp.concatenate([jnp.sin(angles), jnp.cos(angles)], 0).astype(BF16)
    return jnp.dot(w_time, features, preferred_element_type=F32)


def per_device(trajectory, noise, timesteps, w_in, w_time, w_out, well_cells, well_owner, well_values):
    in_hbm = lambda v: pltpu.with_memory_space_constraint(v, pltpu.HBM)
    trajectory, noise = in_hbm(trajectory), in_hbm(noise)
    ranks = jnp.stack([lax.axis_index("tm"), lax.axis_index("space")]).astype(jnp.int32)
    bias = time_bias(w_time, timesteps[:-1])
    rows, top, bottom = pack(in_hbm(well_owner.T), in_hbm(well_cells[None]), in_hbm(well_values.T), trajectory)
    wbig, w2 = call(
        weights_kernel, "weights", 8, [shape(BF16, 2, 512, 256), shape(BF16, 16, 512)],
        [ranks], w_in.T, jnp.asarray(selection(), BF16), bias, w_out,
    )
    rows = lax.all_to_all(rows, "space", 0, 0, tiled=True)
    lo, hi = halos(top, bottom)

    half = shape(F32, 2, C, 4, NX, NY)
    whole = shape(F32, C, ND, NX, NY)
    coded = shape(I16, C, 4, PAY, NY)
    edge = shape(BF16, 2, C, NX, NY)
    s = trajectory
    part = call(inner1_kernel, "inner1", 20, half, [], s, wbig, w2, scratch=CONV_SCRATCH)
    wbig = in_hbm(wbig)
    guide = wells(ranks, rows, part, lo, hi)
    guide = in_hbm(lax.all_to_all(guide, "tm", 0, 0, tiled=True))
    rest = call(outer1_kernel, "outer1", 20, half, [], s, wbig, w2, lo, hi, scratch=CONV_SCRATCH)
    payload, sums = call(
        increments1_kernel, "increments1", 20, [coded, whole], [ranks, timesteps], s, part, rest, noise, guide
    )
    entering = prefix(payload)
    start = trajectory
    lo, hi = halos(*call(edges_kernel, "edges", 8, [edge, edge], [ranks], entering, start, sums, first=[1]))
    part = call(inner2_kernel, "inner2", 20, half, [ranks], entering, start, sums, wbig, w2, scratch=CONV_SCRATCH, first=[1])
    payload, sum0, sum1 = call(
        outer2_kernel, "outer2", 30, [coded, whole, whole], [ranks, timesteps],
        entering, start, sums, wbig, w2, lo, hi, part, noise, guide, first=[1],
        scratch=[pltpu.VMEM(half.shape, F32)] + CONV_SCRATCH,
    )
    return last_states(prefix(payload), sum0, sum1)


def solution(mesh):
    return jax.shard_map(
        per_device,
        mesh=mesh,
        in_specs=(
            P("tm", None, "space", None, None),
            P("tm", None, "space", None, None),
            P(),
            P(),
            P(),
            P(),
            P("space"),
            P("space", None),
            P("space", None),
        ),
        out_specs=P("tm", None, "space", None, None),
        check_vma=False,
    )
```

time: 1250 us -> 154 us (0.12)
  local copies, waits for them, and re-layouts: 434 us -> 0.88 us
  matrix products: 336 us -> 0.2 us
  waiting for transfers between devices: 227 us -> 0.75 us
  other arithmetic: 189 us -> 0.23 us
  blocking collectives: 0 us -> 67.8 us
  Pallas kernels: 0 us -> 64.3 us
  between operations: 18.2 us -> 0.2 us
    conv_general_dilated x32 -> x0, matrix products: 315 us -> none  [one_layer(): lax.conv_general_dilated(slices[None], kernel, (1, 1, 1), [(0, 0), (1, 1)...]
    conv_general_dilated x160 -> x0, local copies, waits for them, and re-layouts: 308 us -> none  [one_layer(): lax.conv_general_dilated(slices[None], kernel, (1, 1, 1), [(0, 0), (1, 1)...]
    all_gather x2 -> x0, waiting for transfers between devices: 227 us -> none  [entering(): pieces = lax.all_gather(value, axis)]
    scatter-add x2 -> x0, other arithmetic: 81.8 us -> none  [the longest x1 53.8 us: per_device(): jnp.zeros((slab_cells + 1, channels), jnp.float32).at[target]]
    all_to_all x0 -> x4, blocking collectives: none -> 67.8 us  [the longest x2 35.9 us: prefix(): got = lax.all_to_all(payload.reshape(TM, PAY, NY), 'tm', 0, 0, tiled=True)]
    pallas_call x0 -> x12, Pallas kernels: none -> 64.3 us  [the longest x9 56.8 us: call(): pl.pallas_call(kernel, grid=(1,), in_specs=[smem()] * len(scalars) + [fir...]
    select_n x33 -> x0, other arithmetic: 48.8 us -> none  [the longest x30 48 us: turn(): return jnp.where(position < mine, longer, so_far)]
    convert_element_type x36 -> x1, other arithmetic: 38.4 us -> 0.01 us  [time_bias(): angles = times.astype(F32)[None, :] * frequency[:, None]]
  transfers between devices with their start and end apart: 12 -> 6, of which waited for: 2 -> 1; matrix products, arithmetic and copies ran while one was open for 42% -> 0% of each run, Pallas kernels for 0% -> 25%
where the time goes in v1:
time: 154 us; the launch traced here: 153 us
  blocking collectives  67.8 us (44%)
  Pallas kernels  64.3 us (42%)
  starting transfers between devices  18.9 us (12%)
    pallas_call x9, Pallas kernels, call(): pl.pallas_call(kernel, grid=(1,), in_specs=[smem()] * len(scalars) + [fir...  56.8 us
    all_to_all x2, blocking collectives, prefix(): got = lax.all_to_all(payload.reshape(TM, PAY, NY), 'tm', 0, 0, tiled=True)  35.9 us
    all_to_all x2, blocking collectives, prefix(): return lax.all_to_all(ahead, 'tm', 0, 0, tiled=True).reshape(C, 4, PAY, NY)  31.9 us
    all_to_all x1, starting transfers between devices, per_device(): guide = in_hbm(lax.all_to_all(guide, 'tm', 0, 0, tiled=True))  7.03 us
    all_to_all x1, starting transfers between devices, per_device(): rows = lax.all_to_all(rows, 'space', 0, 0, tiled=True)  5.43 us
    ppermute x2, starting transfers between devices, halos(): lo = lax.ppermute(bottom, 'space', [(i, i + 1) for i in range(SPACE - 1)])  3.7 us
    pallas_call x1, Pallas kernels, wells(): pl.pallas_call(wells_kernel, grid=(1,), in_specs=[smem(), full(rows.shape...  3.53 us
  transfers between devices with their start and end apart: 6, of which 1 were waited for; matrix products, arithmetic and copies ran while one was open for 0% of the time, Pallas kernels for 25%

profile of v1, /device:TPU:0, one launch (start us, length us, event | category | flops | bytes accessed | tf_op | source)
XLA Modules:
  0.0 153.3 jit_solution(8357870506193996272)
XLA Ops:
  0.0 0.0 copy-start
  0.0 0.0 copy-start.2
  0.0 0.0 copy-start.4
  0.0 0.0 copy-start.5
  0.0 0.0 copy-start.3
  0.0 1.9 %pack.1 = (f32[8,8,1024]{2,1,0:T(8,128)}, bf16[2,4,64,128]{3,2,1,0:T(8,128)(2,1)S(1)}, bf16[2,4,64,128]{3,2,1,0:T(8,128)(2,1)S(1)}) custom-call(s32[1,1024]{1,0:T(1,128)} %bitcast.21, s32[1,1024]{1,0:T(1,128)} %bitcast.22, f32[4,1024]{1,0:T(4,128)} %bitcast.20, f32[2,4,8,64,128]{4,3,2,1,0:T(8,128)} %traj_ref.1), custom_call_target="tpu_custom_call" | custom-call | tf_op jit(solution)/shard_map/pack/pallas_call | solution.py:95
  1.9 5.4 %all-to-all-start = ((f32[8,8,1024]{2,1,0:T(8,128)}), f32[8,8,1024]{2,1,0:T(8,128)S(1)}, u32[]{:S(2)}, u32[]{:S(2)}) async-start(f32[8,8,1024]{2,1,0:T(8,128)} %get-tuple-element.21), calls=%async_computation | async-start | bytes 524288 | tf_op jit(solution)/shard_map/all_to_all | solution.py:446
  7.4 2.4 %collective-permute-start = (bf16[2,4,64,128]{3,2,1,0:T(8,128)(2,1)S(1)}, bf16[2,4,64,128]{3,2,1,0:T(8,128)(2,1)S(1)}, u32[]{:S(2)}, u32[]{:S(2)}) collective-permute-start(bf16[2,4,64,128]{3,2,1,0:T(8,128)(2,1)S(1)} %get-tuple-element.19), channel_id=1, source_target_pairs={{0,1},{1,2},{2,3},{3,4},{4,5},{5,6},{6,7},{8,9},{9,10},{10,11},{11... | collective-permute-start | bytes 393224 | tf_op jit(solution)/shard_map/ppermute | solution.py:423
  9.8 1.3 collective-permute-start.1
  11.1 0.0 copy-done.4
  11.1 0.1 fusion
  11.3 0.0 copy-done
  11.3 0.2 convolution_bitcast_fusion.bias_ref
  11.5 0.1 pad_add_fusion.rank_ref
  11.5 0.0 copy-done.2
  11.5 0.0 copy-done.5
  11.5 0.0 copy-done.3
  11.5 0.8 weights.1
  12.4 0.0 copy-start.1
  12.4 12.4 %inner1.1.refs_0_.in_ref = f32[2,4,4,64,128]{4,3,2,1,0:T(8,128)S(1)} custom-call(f32[2,4,8,64,128]{4,3,2,1,0:T(8,128)} %traj_ref.1, bf16[2,512,256]{2,1,0:T(8,128)(2,1)S(1)} %get-tuple-element.17.wbig, bf16[16,512]{1,0:T(8,128)(2,1)S(1)} %get-tuple-element.18.w2_ref), custom_call_target="tpu_custom_call" | custom-call | tf_op jit(solution)/shard_map/inner1/pallas_call | solution.py:42
  24.8 0.0 collective-permute-done.lo_ref.refs_1_
  24.8 0.0 collective-permute-done.1.hi_ref.refs_2_
  24.8 0.0 all-to-all-done.rows_ref
  24.8 3.5 %wells.1 = s16[16,176,128]{2,1,0:T(8,128)(2,1)} custom-call(s32[2]{0:T(128)S(1)} %pad_add_fusion.rank_ref, f32[8,8,1024]{2,1,0:T(8,128)S(1)} %all-to-all-done.rows_ref, f32[2,4,4,64,128]{4,3,2,1,0:T(8,128)S(1)} %inner1.1.refs_0_.in_ref, bf16[2,4,64,128]{3,2,1,0:T(8,128)(2,1)S(1)} %collective-permute-done.lo_ref.refs_1_, ...), custom_call_target="tpu_custom_call" | custom-call | tf_op jit(solution)/shard_map/wells/pallas_call | solution.py:365
  28.4 0.0 copy-done.1
  28.4 7.0 %all-to-all-start.1 = ((s16[16,176,128]{2,1,0:T(8,128)(2,1)}), s16[16,176,128]{2,1,0:T(8,128)(2,1)S(1)}, u32[]{:S(2)}, u32[]{:S(2)}) async-start(s16[16,176,128]{2,1,0:T(8,128)(2,1)} %wells.1), calls=%async_computation.1 | async-start | bytes 1441792 | tf_op jit(solution)/shard_map/all_to_all | solution.py:457
  35.4 12.4 %outer1.1.out_ref = f32[2,4,4,64,128]{4,3,2,1,0:T(8,128)S(1)} custom-call(f32[2,4,8,64,128]{4,3,2,1,0:T(8,128)} %traj_ref.1, bf16[2,512,256]{2,1,0:T(8,128)(2,1)} %copy-done.1, bf16[16,512]{1,0:T(8,128)(2,1)S(1)} %get-tuple-element.18.w2_ref, bf16[2,4,64,128]{3,2,1,0:T(8,128)(2,1)S(1)} %collective-permute-done.lo_ref.refs_1_, ...), custom_call_target="tpu_custom_call" | custom-call | tf_op jit(solution)/shard_map/outer1/pallas_call | solution.py:42
  47.8 0.7 all-to-all-done.1.g_ref
  48.6 0.0 copy-start.6
  48.6 0.9 copy-done.6
  49.4 3.2 %increments1.1 = (s16[4,4,144,128]{3,2,1,0:T(8,128)(2,1)S(1)}, f32[4,8,64,128]{3,2,1,0:T(8,128)S(1)}) custom-call(s32[2]{0:T(128)S(1)} %pad_add_fusion.rank_ref, s32[33]{0:T(128)S(1)} %copy-done.4, f32[2,4,8,64,128]{4,3,2,1,0:T(8,128)} %traj_ref.1, f32[2,4,4,64,128]{4,3,2,1,0:T(8,128)S(1)} %inner1.1.refs_0_.in_ref, f32[2,4,4,64,128]{4,3,2,1,0:T(8,128)S(1)} %outer1.1.out_ref, ...), custom_call_target="tpu_custom_call" | custom-call | tf_op jit(solution)/shard_map/increments1/pallas_call | solution.py:42
  52.6 19.5 %all_to_all.30.got_ref = s16[16,144,128]{2,1,0:T(8,128)(2,1)S(1)} all-to-all(s16[16,144,128]{2,1,0:T(8,128)(2,1)S(1)} %bitcast.18), channel_id=1, replica_groups=mesh['tm'=16,'space'=8] {'tm'}, dimensions={0} | all-to-all | bytes 1179648 | tf_op jit(solution)/shard_map/all_to_all | solution.py:417
  72.1 0.3 scan.2
  72.4 15.9 %all_to_all.31 = s16[16,144,128]{2,1,0:T(8,128)(2,1)S(1)} all-to-all(s16[16,144,128]{2,1,0:T(8,128)(2,1)S(1)} %scan.2), channel_id=1, replica_groups=mesh['tm'=16,'space'=8] {'tm'}, dimensions={0} | all-to-all | bytes 1179648 | tf_op jit(solution)/shard_map/all_to_all | solution.py:419
  88.3 1.3 edges.1
  89.7 1.3 collective-permute-start.2
  91.0 1.5 collective-permute-start.3
  92.4 12.1 %inner2.1.in_ref = f32[2,4,4,64,128]{4,3,2,1,0:T(8,128)S(1)} custom-call(s32[2]{0:T(128)S(1)} %pad_add_fusion.rank_ref, s16[4,4,144,128]{3,2,1,0:T(8,128)(2,1)S(1)} %bitcast.14, f32[2,4,8,64,128]{4,3,2,1,0:T(8,128)} %traj_ref.1, f32[4,8,64,128]{3,2,1,0:T(8,128)S(1)} %get-tuple-element.23.sum_ref.before_ref, bf16[2,512,256]{2,1,0:T(8,128)(2,1)} %copy-done.1, ...), custom_call_target="tpu_custom_call" | custom-call | tf_op jit(solution)/shard_map/inner2/pallas_call | solution.py:42
  104.5 0.0 collective-permute-done.2.lo_ref
  104.6 0.0 collective-permute-done.3.hi_ref
  104.6 14.0 %outer2.1 = (s16[4,4,144,128]{3,2,1,0:T(8,128)(2,1)S(1)}, f32[4,8,64,128]{3,2,1,0:T(8,128)S(1)}, f32[4,8,64,128]{3,2,1,0:T(8,128)S(1)}) custom-call(s32[2]{0:T(128)S(1)} %pad_add_fusion.rank_ref, s32[33]{0:T(128)S(1)} %copy-done.4, s16[4,4,144,128]{3,2,1,0:T(8,128)(2,1)S(1)} %bitcast.15, f32[2,4,8,64,128]{4,3,2,1,0:T(8,128)} %traj_ref.1, ...), custom_call_target="tpu_custom_call" | custom-call | tf_op jit(solution)/shard_map/outer2/pallas_call | solution.py:42
  118.5 16.5 %all_to_all.32.got_ref = s16[16,144,128]{2,1,0:T(8,128)(2,1)S(1)} all-to-all(s16[16,144,128]{2,1,0:T(8,128)(2,1)S(1)} %bitcast.17), channel_id=1, replica_groups=mesh['tm'=16,'space'=8] {'tm'}, dimensions={0} | all-to-all | bytes 1179648 | tf_op jit(solution)/shard_map/all_to_all | solution.py:417
  135.0 0.3 scan.3
  135.3 15.9 %all_to_all.33 = s16[16,144,128]{2,1,0:T(8,128)(2,1)S(1)} all-to-all(s16[16,144,128]{2,1,0:T(8,128)(2,1)S(1)} %scan.3), channel_id=1, replica_groups=mesh['tm'=16,'space'=8] {'tm'}, dimensions={0} | all-to-all | bytes 1179648 | tf_op jit(solution)/shard_map/all_to_all | solution.py:419
  151.3 2.0 %last_states.1 = f32[2,4,8,64,128]{4,3,2,1,0:T(8,128)} custom-call(s16[4,4,144,128]{3,2,1,0:T(8,128)(2,1)S(1)} %bitcast.16, f32[4,8,64,128]{3,2,1,0:T(8,128)S(1)} %get-tuple-element.27.sum0_ref, f32[4,8,64,128]{3,2,1,0:T(8,128)S(1)} %get-tuple-element.28.sum1_ref), custom_call_target="tpu_custom_call" | custom-call | tf_op jit(solution)/shard_map/last_states/pallas_call | solution.py:324
  (2 shorter events, 0.0 us)
Async XLA Ops:
  0.0 11.3 %copy-start = (bf16[128,128]{1,0:T(8,128)(2,1)S(1)}, bf16[128,128]{1,0:T(8,128)(2,1)}, u32[]{:S(2)}) copy-start(bf16[128,128]{1,0:T(8,128)(2,1)} %param.14) | copy-start | bytes 98308
  0.0 11.5 %copy-start.2 = (bf16[4,108,256]{2,1,0:T(8,128)(2,1)S(1)}, bf16[4,108,256]{2,1,0:T(8,128)(2,1)}, u32[]{:S(2)}) copy-start(bf16[4,108,256]{2,1,0:T(8,128)(2,1)} %constant.16.clone.sel_ref) | copy-start | bytes 663556
  0.0 11.1 %copy-start.4 = (s32[33]{0:T(128)S(1)}, s32[33]{0:T(128)}, u32[]{:S(2)}) copy-start(s32[33]{0:T(128)} %ts_ref.3) | copy-start | bytes 400
  0.0 11.5 %copy-start.5 = (bf16[4,128]{1,0:T(4,128)(2,1)S(1)}, bf16[4,128]{1,0:T(4,128)(2,1)}, u32[]{:S(2)}) copy-start(bf16[4,128]{1,0:T(4,128)(2,1)} %out_ref.1) | copy-start | bytes 3076
  0.0 11.5 %copy-start.3 = (bf16[128,108]{0,1:T(8,128)(2,1)S(1)}, bf16[128,108]{0,1:T(8,128)(2,1)}, u32[]{:S(2)}) copy-start(bf16[128,108]{0,1:T(8,128)(2,1)} %param.13) | copy-start | bytes 82948
  1.9 22.9 %all-to-all-start = ((f32[8,8,1024]{2,1,0:T(8,128)}), f32[8,8,1024]{2,1,0:T(8,128)S(1)}, u32[]{:S(2)}, u32[]{:S(2)}) async-start(f32[8,8,1024]{2,1,0:T(8,128)} %get-tuple-element.21), calls=%async_computation | async-start | bytes 524288 | tf_op jit(solution)/shard_map/all_to_all | solution.py:446
  7.4 17.5 %collective-permute-start = (bf16[2,4,64,128]{3,2,1,0:T(8,128)(2,1)S(1)}, bf16[2,4,64,128]{3,2,1,0:T(8,128)(2,1)S(1)}, u32[]{:S(2)}, u32[]{:S(2)}) collective-permute-start(bf16[2,4,64,128]{3,2,1,0:T(8,128)(2,1)S(1)} %get-tuple-element.19), channel_id=1, source_target_pairs={{0,1},{1,2},{2,3},{3,4},{4,5},{5,6},{6,7},{8,9},{9,10},{10,11},{11... | collective-permute-start | bytes 393224 | tf_op jit(solution)/shard_map/ppermute | solution.py:423
  9.8 15.1 %collective-permute-start.1 = (bf16[2,4,64,128]{3,2,1,0:T(8,128)(2,1)S(1)}, bf16[2,4,64,128]{3,2,1,0:T(8,128)(2,1)S(1)}, u32[]{:S(2)}, u32[]{:S(2)}) collective-permute-start(bf16[2,4,64,128]{3,2,1,0:T(8,128)(2,1)S(1)} %get-tuple-element.20), channel_id=1, source_target_pairs={{1,0},{2,1},{3,2},{4,3},{5,4},{6,5},{7,6},{9,8},{10,9},{11,10},{12... | collective-permute-start | bytes 393224 | tf_op jit(solution)/shard_map/ppermute | solution.py:424
  12.4 16.0 %copy-start.1 = (bf16[2,512,256]{2,1,0:T(8,128)(2,1)}, bf16[2,512,256]{2,1,0:T(8,128)(2,1)S(1)}, u32[]{:S(2)}) copy-start(bf16[2,512,256]{2,1,0:T(8,128)(2,1)S(1)} %get-tuple-element.17.wbig) | copy-start | bytes 1572868
  28.4 20.2 %all-to-all-start.1 = ((s16[16,176,128]{2,1,0:T(8,128)(2,1)}), s16[16,176,128]{2,1,0:T(8,128)(2,1)S(1)}, u32[]{:S(2)}, u32[]{:S(2)}) async-start(s16[16,176,128]{2,1,0:T(8,128)(2,1)} %wells.1), calls=%async_computation.1 | async-start | bytes 1441792 | tf_op jit(solution)/shard_map/all_to_all | solution.py:457
  48.6 0.9 copy-start.6
  89.7 14.9 %collective-permute-start.2 = (bf16[2,4,64,128]{3,2,1,0:T(8,128)(2,1)S(1)}, bf16[2,4,64,128]{3,2,1,0:T(8,128)(2,1)S(1)}, u32[]{:S(2)}, u32[]{:S(2)}) collective-permute-start(bf16[2,4,64,128]{3,2,1,0:T(8,128)(2,1)S(1)} %get-tuple-element.24), channel_id=1, source_target_pairs={{0,1},{1,2},{2,3},{3,4},{4,5},{5,6},{6,7},{8,9},{9,10},{10,11},{11... | collective-permute-start | bytes 393224 | tf_op jit(solution)/shard_map/ppermute | solution.py:423
  91.0 13.6 %collective-permute-start.3 = (bf16[2,4,64,128]{3,2,1,0:T(8,128)(2,1)S(1)}, bf16[2,4,64,128]{3,2,1,0:T(8,128)(2,1)S(1)}, u32[]{:S(2)}, u32[]{:S(2)}) collective-permute-start(bf16[2,4,64,128]{3,2,1,0:T(8,128)(2,1)S(1)} %get-tuple-element.25), channel_id=1, source_target_pairs={{1,0},{2,1},{3,2},{4,3},{5,4},{6,5},{7,6},{9,8},{10,9},{11,10},{12... | collective-permute-start | bytes 393224 | tf_op jit(solution)/shard_map/ppermute | solution.py:424

commit v2 on v1

--- a/solution.py
+++ b/solution.py
@@ -16,9 +16,9 @@
 GUIDE_GAIN = 2.0
 NOISE_COEF = 0.5
 TIME_SCALE = 500.0
-EXP = 16
+EXP = 8
 PAY = 2 * NX + EXP
-GPAY = 5 * 32 + EXP
+GPAY = 5 * 32 + 16
 MIB = 2**20
 
 
@@ -34,21 +34,62 @@
     return pl.BlockSpec(dims, lambda i: (0,) * len(dims), pipeline_mode=pl.Buffered(1))
 
 
-def first_step(v):
-    return pl.BlockSpec((1,) + v.shape[1:], lambda i: (0,) * v.ndim, pipeline_mode=pl.Buffered(1))
-
-
-def call(kernel, name, mib, out_shape, scalars, *args, scratch=(), first=()):
+def in_hbm(value):
+    return pltpu.with_memory_space_constraint(value, pltpu.HBM)
+
+
+class Hbm:
+    def __init__(self, value):
+        self.value = in_hbm(value)
+
+
+class Anywhere:
+    def __init__(self, value):
+        self.value = value
+
+
+class First:
+    def __init__(self, value):
+        self.value = in_hbm(value)
+
+
+def spec_of(v):
+    if isinstance(v, Hbm):
+        return pl.BlockSpec(memory_space=pltpu.HBM)
+    if isinstance(v, Anywhere):
+        return pl.BlockSpec(memory_space=pl.ANY)
+    if isinstance(v, First):
+        dims = v.value.shape
+        return pl.BlockSpec((1,) + dims[1:], lambda i: (0,) * len(dims), pipeline_mode=pl.Buffered(1))
+    return full(v.shape)
+
+
+def call(kernel, name, mib, out_shape, scalars, *args, scratch=()):
     return pl.pallas_call(
         kernel,
         grid=(1,),
-        in_specs=[smem()] * len(scalars) + [first_step(v) if i in first else full(v.shape) for i, v in enumerate(args)],
+        in_specs=[smem()] * len(scalars) + [spec_of(v) for v in args],
         out_specs=jax.tree.map(lambda v: full(v.shape), out_shape),
         out_shape=out_shape,
         scratch_shapes=list(scratch),
         compiler_params=params(mib),
         name=name,
-    )(*scalars, *args)
+    )(*scalars, *[v.value if isinstance(v, (Hbm, Anywhere, First)) else v for v in args])
+
+
+class Loads:
+    def __init__(self, sems, **groups):
+        self.copies, at = {}, 0
+        for name, pairs in groups.items():
+            self.copies[name] = [pltpu.make_async_copy(src, dst, sems.at[at + i]) for i, (src, dst) in enumerate(pairs)]
+            at += len(pairs)
+        for copies in self.copies.values():
+            for copy in copies:
+                copy.start()
+
+    def wait(self, name):
+        for copy in self.copies.pop(name, []):
+            copy.wait()
 
 
 def shape(dtype, *dims):
@@ -131,29 +172,29 @@
 
 INNER, OUTER = (1, 2), (0, 3)
 CONV_SCRATCH = [
-    pltpu.VMEM((NX * 40, NY), F32),
-    pltpu.VMEM((2, 66 * 48, NY), BF16),
+    pltpu.VMEM((2, 512, 256), BF16),
+    pltpu.VMEM(((NX + 9) * 40, NY), F32),
+    pltpu.VMEM((2, (NX + 10) * 48, NY), BF16),
     pltpu.VMEM((72 * 16, NY), F32),
     pltpu.VMEM((4, 512, 256), BF16),
     pltpu.VMEM((4, 512, 256), BF16),
 ]
 
 
-def clear(Q, HB):
-    zt = jnp.zeros((48, NY), BF16)
+def clear(S, Q, HB):
+    S[NX * 40:(NX + 9) * 40, :] = jnp.zeros((9 * 40, NY), F32)
     for i in range(2):
-        Q[i, 0:48, :] = zt
-        Q[i, 65 * 48:66 * 48, :] = zt
+        Q[i, 0:48, :] = jnp.zeros((48, NY), BF16)
     HB[...] = jnp.zeros(HB.shape, BF16)
 
 
-def conv_step(layer, pairs, wbig, w2_ref, put, S, Q, So, HA, HB):
+def conv_step(layer, pairs, wbig, w2_ref, put, S, Q, So, HA, HB, ready):
     for dp in sorted({2 * p + i for p in pairs for i in range(4)}):
         for c in range(C):
             S[pl.ds(dp * 4 + c, NX, stride=40), :] = layer(c, dp)
     lane = lax.broadcasted_iota(jnp.int32, (16, NY), 1)
 
-    def prep(x, carry):
+    def prep(x):
         base = pl.multiple_of((x + 1) * 48, 16)
         for i, p in enumerate(pairs):
             v = S[pl.ds(pl.multiple_of(x * 40 + 8 * p, 8), 16), :]
@@ -164,9 +205,10 @@
             ]
             for e in range(3):
                 Q[i, pl.ds(base + 16 * e, 16), :] = ve[e].astype(BF16)
-        return carry
-
-    lax.fori_loop(0, NX, prep, 0, unroll=8)
+
+    for x in range(9):
+        prep(x)
+    ready()
     ones = jnp.ones((16, 256), BF16)
 
     def first(t, hidden):
@@ -178,6 +220,8 @@
             patch = jnp.concatenate([jnp.concatenate([pa, pb], 1), ones], 0)
             u = jnp.dot(wbig[:, 0:208], patch, preferred_element_type=F32)
             hidden[g] = (u + u * jnp.tanh(u)).astype(BF16)
+            for k in range(2):
+                prep(8 * t + 9 + 2 * g + k)
             yield
 
     def second(t, hidden):
@@ -206,39 +250,25 @@
                 put(c, 2 * i + dd, So[pl.ds(128 + i * 8 + dd * 4 + c, NX, stride=16), :])
 
 
-def inner(state, wbig, w2_ref, o_ref, scratch):
-    clear(scratch[1], scratch[4])
+def convolve(state, pairs, halo, w2_ref, put, loads, scratch):
+    wbig, S, Q, So, HA, HB = scratch
+    clear(S, Q, HB)
+
+    def layer(j, c, dp):
+        if dp in (0, ND + 1):
+            return halo[dp > 0][j, c].astype(F32)
+        return state(j, c, dp - 1)
+
     for j in range(2):
+        loads.wait(f"step{j}")
         conv_step(
-            lambda c, dp: state(j, c, dp - 1), INNER, wbig.at[j], w2_ref,
-            lambda c, i, v: o_ref.__setitem__((j, c, i), v), *scratch,
+            lambda c, dp: layer(j, c, dp), pairs, wbig.at[j], w2_ref, lambda c, i, v: put(j, c, i, v),
+            S, Q, So, HA, HB, lambda: loads.wait("weights"),
         )
 
 
-def outer(state, wbig, w2_ref, lo_ref, hi_ref, o_ref, scratch):
-    clear(scratch[1], scratch[4])
-
-    def layer(j, c, dp):
-        if dp == 0:
-            return lo_ref[j, c].astype(F32)
-        if dp == ND + 1:
-            return hi_ref[j, c].astype(F32)
-        return state(j, c, dp - 1)
-
-    for j in range(2):
-        conv_step(
-            lambda c, dp: layer(j, c, dp), OUTER, wbig.at[j], w2_ref,
-            lambda c, i, v: o_ref.__setitem__((j, c, i), v), *scratch,
-        )
-
-
 def increments(state, rank_ref, ts_ref, in_ref, out_ref, n_ref, g_ref, start, pay_ref, sums_refs):
-    tm = rank_ref[0]
-    step, gain = [], []
-    for j in range(2):
-        span = jnp.full((1, NY), ts_ref[2 * tm + j] - ts_ref[2 * tm + j + 1], jnp.int32).astype(F32) / TIME_SCALE
-        step.append(span)
-        gain.append(jnp.sqrt(span) * NOISE_COEF)
+    step, gain = gains(rank_ref, ts_ref)
     for p in range(4):
         for c in range(C):
             totals = []
@@ -274,30 +304,94 @@
     return state
 
 
-def inner1_kernel(s_ref, wbig, w2_ref, o_ref, *scratch):
-    inner(given(s_ref), wbig, w2_ref, o_ref, scratch)
-
-
-def inner2_kernel(rank_ref, e_ref, start_ref, sum_ref, wbig, w2_ref, o_ref, *scratch):
-    inner(arrived(e_ref, first_of(rank_ref, start_ref.at[0]), sum_ref), wbig, w2_ref, o_ref, scratch)
-
-
-def outer1_kernel(s_ref, wbig, w2_ref, lo_ref, hi_ref, o_ref, *scratch):
-    outer(given(s_ref), wbig, w2_ref, lo_ref, hi_ref, o_ref, scratch)
+def inner1_kernel(s_hbm, wbig_hbm, w2_ref, o_ref, s, sems, *scratch):
+    loads = Loads(
+        sems, step0=[(s_hbm.at[0, :, 1:7], s.at[0])], weights=[(wbig_hbm, scratch[0])], step1=[(s_hbm.at[1, :, 1:7], s.at[1])]
+    )
+    put = lambda j, c, i, v: o_ref.__setitem__((j, c, i), v)
+    convolve(lambda j, c, d: s[j, c, d - 1], INNER, None, w2_ref, put, loads, scratch)
+
+
+def outer1_kernel(s_hbm, wbig_hbm, w2_ref, lo_ref, hi_ref, o_ref, s, sems, *scratch):
+    step = lambda j: [(s_hbm.at[j, :, 0:3], s.at[j, :, 0:3]), (s_hbm.at[j, :, 5:8], s.at[j, :, 3:6])]
+    loads = Loads(sems, step0=step(0), weights=[(wbig_hbm, scratch[0])], step1=step(1))
+    put = lambda j, c, i, v: o_ref.__setitem__((j, c, i), v)
+    state = lambda j, c, d: s[j, c, d if d < 3 else d - 2]
+    convolve(state, OUTER, (lo_ref, hi_ref), w2_ref, put, loads, scratch)
+
+
+def gains(rank_ref, ts_ref):
+    tm = rank_ref[0]
+    step, gain = [], []
+    for j in range(2):
+        span = jnp.full((1, NY), ts_ref[2 * tm + j] - ts_ref[2 * tm + j + 1], jnp.int32).astype(F32) / TIME_SCALE
+        step.append(span)
+        gain.append(jnp.sqrt(span) * NOISE_COEF)
+    return step, gain
 
 
 def increments1_kernel(rank_ref, ts_ref, s_ref, in_ref, out_ref, n_ref, g_ref, pay_ref, sum_ref):
-    start = first_of(rank_ref, s_ref.at[0])
-    increments(given(s_ref), rank_ref, ts_ref, in_ref, out_ref, n_ref, g_ref, start, pay_ref, [sum_ref])
+    step, gain = gains(rank_ref, ts_ref)
+    keep = jnp.where(rank_ref[0] == 0, 1.0, 0.0)
+    pair = pl.program_id(0)
+    is_inner = jnp.logical_or(pair == 1, pair == 2)
+    for c in range(C):
+        totals = []
+        for dd in range(2):
+            observed, count = guide_at(g_ref, dd, c)
+            total = keep * s_ref[0, c, dd]
+            for j in range(2):
+                drift = jnp.where(is_inner, in_ref[j, c, dd], out_ref[j, c, dd])
+                drift = drift + GUIDE_GAIN * (observed - count * s_ref[j, c, dd])
+                total = total + step[j] * drift + gain[j] * n_ref[j, c, dd].astype(F32)
+                if j == 0:
+                    sum_ref[c, dd] = total
+            totals.append(total)
+        encode(totals, lambda at, n, v: pay_ref.__setitem__((c, pl.ds(at, n), slice(None)), v))
+
+
+def increments1(ranks, timesteps, s, inner, outer, noise, guide):
+    pair = lambda place: pl.BlockSpec((2, C, 2, NX, NY), lambda p: (0, 0, place(p), 0, 0))
+    return pl.pallas_call(
+        increments1_kernel,
+        grid=(4,),
+        in_specs=[
+            smem(), smem(), pair(lambda p: p), pair(lambda p: p // 2), pair(lambda p: p // 2), pair(lambda p: p),
+            pl.BlockSpec((4, GPAY, NY), lambda p: (p, 0, 0)),
+        ],
+        out_specs=[
+            pl.BlockSpec((C, None, PAY, NY), lambda p: (0, p, 0, 0)),
+            pl.BlockSpec((C, 2, NX, NY), lambda p: (0, p, 0, 0)),
+        ],
+        out_shape=[shape(I16, C, 4, PAY, NY), shape(F32, C, ND, NX, NY)],
+        compiler_params=params(16),
+        name="increments1",
+    )(ranks, timesteps, s, inner, outer, noise, guide)
+
+
+def inner2_kernel(rank_ref, e_ref, traj_hbm, before_hbm, wbig_hbm, w2_ref, o_ref, traj, before, sems, *scratch):
+    loads = Loads(
+        sems, step0=[(traj_hbm.at[0, :, 1:7], traj.at[0, :, 1:7])], weights=[(wbig_hbm, scratch[0])],
+        step1=[(before_hbm.at[:, 1:7], before.at[:, 1:7])],
+    )
+    state = arrived(e_ref, first_of(rank_ref, traj.at[0]), before)
+    put = lambda j, c, i, v: o_ref.__setitem__((j, c, i), v)
+    convolve(state, INNER, None, w2_ref, put, loads, scratch)
 
 
 def outer2_kernel(
-    rank_ref, ts_ref, e_ref, traj_ref, before_ref, wbig, w2_ref, lo_ref, hi_ref, in_ref, n_ref, g_ref,
-    pay_ref, sum0_ref, sum1_ref, out_ref, *scratch,
+    rank_ref, ts_ref, e_ref, lo_ref, hi_ref, w2_ref, traj_hbm, before_hbm, wbig_hbm, in_hbm_ref, n_hbm, g_hbm,
+    pay_ref, sum0_ref, sum1_ref, traj, before, in_ref, n_ref, g_ref, out_ref, sems, *scratch,
 ):
-    start = first_of(rank_ref, traj_ref.at[0])
-    state = arrived(e_ref, start, before_ref)
-    outer(state, wbig, w2_ref, lo_ref, hi_ref, out_ref, scratch)
+    loads = Loads(
+        sems, step0=[(traj_hbm.at[0:1], traj)], weights=[(wbig_hbm, scratch[0])], step1=[(before_hbm, before)],
+        late=[(n_hbm, n_ref), (g_hbm, g_ref), (in_hbm_ref, in_ref)],
+    )
+    start = first_of(rank_ref, traj.at[0])
+    state = arrived(e_ref, start, before)
+    put = lambda j, c, i, v: out_ref.__setitem__((j, c, i), v)
+    convolve(state, OUTER, (lo_ref, hi_ref), w2_ref, put, loads, scratch)
+    loads.wait("late")
     increments(state, rank_ref, ts_ref, in_ref, out_ref, n_ref, g_ref, start, pay_ref, [sum0_ref, sum1_ref])
 
 
@@ -355,7 +449,7 @@
         total = total + lax.dot_general(left, right, (((1,), (1,)), ((), ())), preferred_element_type=F32)
     observed = [total[at:at + 32] + total[at + 32:at + 64] + total[at + 64:at + 96] for at in range(32, 13 * 32, 96)]
     power, factor = power_of(observed)
-    pieces = [jnp.round(v * factor) for v in observed] + [total[0:32], jnp.broadcast_to(power, (EXP, NY))]
+    pieces = [jnp.round(v * factor) for v in observed] + [total[0:32], jnp.broadcast_to(power, (16, NY))]
     coded = jnp.concatenate(pieces, 0).astype(jnp.int32).astype(I16)
     for k in range(TM):
         o_ref[k] = coded
@@ -377,7 +471,7 @@
     observed, count = [], []
     for k in (2 * d, 2 * d + 1):
         wide = lambda at, n: g_ref[k, pl.ds(at, n), :].astype(jnp.int32).astype(F32)
-        observed.append(wide(c * 32, 32) * jnp.exp2(wide(5 * 32, EXP)[0:1]))
+        observed.append(wide(c * 32, 32) * jnp.exp2(wide(5 * 32, 16)[0:1]))
         count.append(wide(4 * 32, 32))
     return jnp.concatenate(observed, 0), jnp.concatenate(count, 0)
 
@@ -434,11 +528,9 @@
 
 
 def per_device(trajectory, noise, timesteps, w_in, w_time, w_out, well_cells, well_owner, well_values):
-    in_hbm = lambda v: pltpu.with_memory_space_constraint(v, pltpu.HBM)
-    trajectory, noise = in_hbm(trajectory), in_hbm(noise)
     ranks = jnp.stack([lax.axis_index("tm"), lax.axis_index("space")]).astype(jnp.int32)
     bias = time_bias(w_time, timesteps[:-1])
-    rows, top, bottom = pack(in_hbm(well_owner.T), in_hbm(well_cells[None]), in_hbm(well_values.T), trajectory)
+    rows, top, bottom = pack(in_hbm(well_owner.T), in_hbm(well_cells[None]), in_hbm(well_values.T), in_hbm(trajectory))
     wbig, w2 = call(
         weights_kernel, "weights", 8, [shape(BF16, 2, 512, 256), shape(BF16, 16, 512)],
         [ranks], w_in.T, jnp.asarray(selection(), BF16), bias, w_out,
@@ -450,23 +542,29 @@
     whole = shape(F32, C, ND, NX, NY)
     coded = shape(I16, C, 4, PAY, NY)
     edge = shape(BF16, 2, C, NX, NY)
-    s = trajectory
-    part = call(inner1_kernel, "inner1", 20, half, [], s, wbig, w2, scratch=CONV_SCRATCH)
-    wbig = in_hbm(wbig)
+    vm = lambda *dims: pltpu.VMEM(dims, F32)
+    six = vm(2, C, 6, NX, NY)
+    sems = lambda n: pltpu.SemaphoreType.DMA((n,))
+    s, wbig = Hbm(trajectory), Anywhere(wbig)
+    part = call(inner1_kernel, "inner1", 20, half, [], s, wbig, w2, scratch=[six, sems(3)] + CONV_SCRATCH)
     guide = wells(ranks, rows, part, lo, hi)
-    guide = in_hbm(lax.all_to_all(guide, "tm", 0, 0, tiled=True))
-    rest = call(outer1_kernel, "outer1", 20, half, [], s, wbig, w2, lo, hi, scratch=CONV_SCRATCH)
-    payload, sums = call(
-        increments1_kernel, "increments1", 20, [coded, whole], [ranks, timesteps], s, part, rest, noise, guide
-    )
+    guide = lax.all_to_all(guide, "tm", 0, 0, tiled=True)
+    rest = call(outer1_kernel, "outer1", 20, half, [], s, wbig, w2, lo, hi, scratch=[six, sems(5)] + CONV_SCRATCH)
+    payload, sums = increments1(ranks, timesteps, s.value, part, rest, in_hbm(noise), guide)
     entering = prefix(payload)
-    start = trajectory
-    lo, hi = halos(*call(edges_kernel, "edges", 8, [edge, edge], [ranks], entering, start, sums, first=[1]))
-    part = call(inner2_kernel, "inner2", 20, half, [ranks], entering, start, sums, wbig, w2, scratch=CONV_SCRATCH, first=[1])
+    lo, hi = halos(*call(edges_kernel, "edges", 8, [edge, edge], [ranks], entering, First(trajectory), sums))
+    sums = Anywhere(sums)
+    part = call(
+        inner2_kernel, "inner2", 20, half, [ranks], entering, s, sums, wbig, w2,
+        scratch=[vm(1, C, ND, NX, NY), vm(C, ND, NX, NY), sems(3)] + CONV_SCRATCH,
+    )
     payload, sum0, sum1 = call(
-        outer2_kernel, "outer2", 30, [coded, whole, whole], [ranks, timesteps],
-        entering, start, sums, wbig, w2, lo, hi, part, noise, guide, first=[1],
-        scratch=[pltpu.VMEM(half.shape, F32)] + CONV_SCRATCH,
+        outer2_kernel, "outer2", 32, [coded, whole, whole], [ranks, timesteps],
+        entering, lo, hi, w2, s, sums, wbig, Anywhere(part), Hbm(noise), Anywhere(guide),
+        scratch=[
+            vm(1, C, ND, NX, NY), vm(C, ND, NX, NY), vm(*half.shape), pltpu.VMEM((2, C, ND, NX, NY), BF16),
+            pltpu.VMEM((TM, GPAY, NY), I16), vm(*half.shape), sems(6),
+        ] + CONV_SCRATCH,
     )
     return last_states(prefix(payload), sum0, sum1)
 

time: 154 us -> 147 us (0.955)
  Pallas kernels: 64.3 us -> 58.6 us
  blocking collectives: 67.8 us -> 65.5 us
    pallas_call x9, Pallas kernels: 56.8 us -> 51.1 us  [the longest x8 47.5 us: call(): pl.pallas_call(kernel, grid=(1,), in_specs=[smem()] * len(scalars) + [spe...]
    all_to_all x2, blocking collectives: 35.9 us -> 34.4 us  [prefix(): got = lax.all_to_all(payload.reshape(TM, PAY, NY), 'tm', 0, 0, tiled=True)]
  transfers between devices with their start and end apart: 6 -> 6, of which waited for: 1 -> 1; matrix products, arithmetic and copies ran while one was open for 0% -> 0% of each run, Pallas kernels for 25% -> 23%
where the time goes in v2:
time: 147 us; the launch traced here: 146 us
  blocking collectives  65.5 us (45%)
  Pallas kernels  58.6 us (40%)
  starting transfers between devices  18.9 us (13%)
  waiting for transfers between devices  1.77 us (1%)
    pallas_call x8, Pallas kernels, call(): pl.pallas_call(kernel, grid=(1,), in_specs=[smem()] * len(scalars) + [spe...  47.5 us
    all_to_all x2, blocking collectives, prefix(): got = lax.all_to_all(payload.reshape(TM, PAY, NY), 'tm', 0, 0, tiled=True)  34.4 us
    all_to_all x2, blocking collectives, prefix(): return lax.all_to_all(ahead, 'tm', 0, 0, tiled=True).reshape(C, 4, PAY, NY)  31.1 us
    all_to_all x1, starting transfers between devices, per_device(): guide = lax.all_to_all(guide, 'tm', 0, 0, tiled=True)  7.03 us
    all_to_all x1, starting transfers between devices, per_device(): rows = lax.all_to_all(rows, 'space', 0, 0, tiled=True)  5.43 us
    ppermute x2, starting transfers between devices, halos(): lo = lax.ppermute(bottom, 'space', [(i, i + 1) for i in range(SPACE - 1)])  3.7 us
    pallas_call x1, Pallas kernels, increments1(): pl.pallas_call(increments1_kernel, grid=(4,), in_specs=[smem(), smem(), p...  3.56 us
    pallas_call x1, Pallas kernels, wells(): pl.pallas_call(wells_kernel, grid=(1,), in_specs=[smem(), full(rows.shape...  3.53 us
  transfers between devices with their start and end apart: 6, of which 1 were waited for; matrix products, arithmetic and copies ran while one was open for 0% of the time, Pallas kernels for 23%

profile of v2, /device:TPU:0, one launch (start us, length us, event | category | flops | bytes accessed | tf_op | source)
XLA Modules:
  0.0 146.3 jit_solution(4815000611600733485)
XLA Ops:
  0.0 0.0 copy-start
  0.0 0.0 copy-start.3
  0.0 0.0 copy-start.5
  0.0 0.0 copy-start.6
  0.0 0.0 copy-start.4
  0.0 1.9 %pack.1 = (f32[8,8,1024]{2,1,0:T(8,128)}, bf16[2,4,64,128]{3,2,1,0:T(8,128)(2,1)S(1)}, bf16[2,4,64,128]{3,2,1,0:T(8,128)(2,1)S(1)}) custom-call(s32[1,1024]{1,0:T(1,128)} %bitcast.21, s32[1,1024]{1,0:T(1,128)} %bitcast.22, f32[4,1024]{1,0:T(4,128)} %bitcast.20, f32[2,4,8,64,128]{4,3,2,1,0:T(8,128)} %traj_hbm.5), custom_call_target="tpu_custom_call" | custom-call | tf_op jit(solution)/shard_map/pack/pallas_call | solution.py:136
  1.9 5.4 %all-to-all-start = ((f32[8,8,1024]{2,1,0:T(8,128)}), f32[8,8,1024]{2,1,0:T(8,128)S(1)}, u32[]{:S(2)}, u32[]{:S(2)}) async-start(f32[8,8,1024]{2,1,0:T(8,128)} %get-tuple-element.21), calls=%async_computation | async-start | bytes 524288 | tf_op jit(solution)/shard_map/all_to_all | solution.py:538
  7.4 2.4 %collective-permute-start = (bf16[2,4,64,128]{3,2,1,0:T(8,128)(2,1)S(1)}, bf16[2,4,64,128]{3,2,1,0:T(8,128)(2,1)S(1)}, u32[]{:S(2)}, u32[]{:S(2)}) collective-permute-start(bf16[2,4,64,128]{3,2,1,0:T(8,128)(2,1)S(1)} %get-tuple-element.19), channel_id=1, source_target_pairs={{0,1},{1,2},{2,3},{3,4},{4,5},{5,6},{6,7},{8,9},{9,10},{10,11},{11... | collective-permute-start | bytes 393224 | tf_op jit(solution)/shard_map/ppermute | solution.py:517
  9.8 1.3 collective-permute-start.1
  11.1 0.0 copy-done.5
  11.1 0.1 fusion
  11.3 0.0 copy-done
  11.3 0.2 convolution_bitcast_fusion.bias_ref
  11.5 0.1 pad_add_fusion.rank_ref
  11.5 0.0 copy-done.3
  11.5 0.0 copy-done.6
  11.5 0.0 copy-done.4
  11.5 0.8 weights.1
  12.4 10.5 %inner1.1.refs_0_.in_ref = f32[2,4,4,64,128]{4,3,2,1,0:T(8,128)S(1)} custom-call(f32[2,4,8,64,128]{4,3,2,1,0:T(8,128)} %traj_hbm.5, bf16[2,512,256]{2,1,0:T(8,128)(2,1)S(1)} %get-tuple-element.17.wbig_hbm, bf16[16,512]{1,0:T(8,128)(2,1)S(1)} %get-tuple-element.18.w2_ref), custom_call_target="tpu_custom_call" | custom-call | tf_op jit(solution)/shard_map/inner1/pallas_call | solution.py:68
  22.9 0.0 collective-permute-done.lo_ref.refs_1_
  22.9 0.0 collective-permute-done.1.hi_ref.refs_2_
  22.9 0.0 copy-start.1
  22.9 0.0 all-to-all-done.rows_ref
  23.0 3.5 %wells.1 = s16[16,176,128]{2,1,0:T(8,128)(2,1)} custom-call(s32[2]{0:T(128)S(1)} %pad_add_fusion.rank_ref, f32[8,8,1024]{2,1,0:T(8,128)S(1)} %all-to-all-done.rows_ref, f32[2,4,4,64,128]{4,3,2,1,0:T(8,128)S(1)} %inner1.1.refs_0_.in_ref, bf16[2,4,64,128]{3,2,1,0:T(8,128)(2,1)S(1)} %collective-permute-done.lo_ref.refs_1_, ...), custom_call_target="tpu_custom_call" | custom-call | tf_op jit(solution)/shard_map/wells/pallas_call | solution.py:459
  26.5 0.0 copy-done.1
  26.5 7.0 %all-to-all-start.1 = ((s16[16,176,128]{2,1,0:T(8,128)(2,1)}), s16[16,176,128]{2,1,0:T(8,128)(2,1)S(1)}, u32[]{:S(2)}, u32[]{:S(2)}) async-start(s16[16,176,128]{2,1,0:T(8,128)(2,1)} %wells.1), calls=%async_computation.1 | async-start | bytes 1441792 | tf_op jit(solution)/shard_map/all_to_all | solution.py:551
  33.5 0.0 copy-start.2
  33.5 0.9 copy-done.2
  34.4 10.5 %outer1.1.out_ref = f32[2,4,4,64,128]{4,3,2,1,0:T(8,128)S(1)} custom-call(f32[2,4,8,64,128]{4,3,2,1,0:T(8,128)} %traj_hbm.5, bf16[2,512,256]{2,1,0:T(8,128)(2,1)S(1)} %get-tuple-element.17.wbig_hbm, bf16[16,512]{1,0:T(8,128)(2,1)S(1)} %get-tuple-element.18.w2_ref, bf16[2,4,64,128]{3,2,1,0:T(8,128)(2,1)S(1)} %collective-permute-done.lo_ref.refs_1_, ...), custom_call_target="tpu_custom_call" | custom-call | tf_op jit(solution)/shard_map/outer1/pallas_call | solution.py:68
  44.9 1.8 %all-to-all-done.1.g_ref.g_hbm = s16[16,176,128]{2,1,0:T(8,128)(2,1)S(1)} async-done(((s16[16,176,128]{2,1,0:T(8,128)(2,1)}), s16[16,176,128]{2,1,0:T(8,128)(2,1)S(1)}, u32[]{:S(2)}, u32[]{:S(2)}) %all-to-all-start.1) | async-done | bytes 720928 | tf_op jit(solution)/shard_map/all_to_all | solution.py:551
  46.7 3.6 %increments1.1 = (s16[4,4,136,128]{3,2,1,0:T(8,128)(2,1)S(1)}, f32[4,8,64,128]{3,2,1,0:T(8,128)S(1)}) custom-call(s32[2]{0:T(128)S(1)} %pad_add_fusion.rank_ref, s32[33]{0:T(128)S(1)} %copy-done.5, f32[2,4,8,64,128]{4,3,2,1,0:T(8,128)} %traj_hbm.5, f32[2,4,4,64,128]{4,3,2,1,0:T(8,128)S(1)} %inner1.1.refs_0_.in_ref, f32[2,4,4,64,128]{4,3,2,1,0:T(8,128)S(1)} %outer1.1.out_ref, ...), custom_call_target="tpu_custom_call" | custom-call | tf_op jit(solution)/shard_map/increments1/pallas_call | solution.py:355
  50.2 18.3 %all_to_all.30.got_ref = s16[16,136,128]{2,1,0:T(8,128)(2,1)S(1)} all-to-all(s16[16,136,128]{2,1,0:T(8,128)(2,1)S(1)} %bitcast.18), channel_id=1, replica_groups=mesh['tm'=16,'space'=8] {'tm'}, dimensions={0} | all-to-all | bytes 1114112 | tf_op jit(solution)/shard_map/all_to_all | solution.py:511
  68.5 0.3 scan.2
  68.8 15.6 %all_to_all.31 = s16[16,136,128]{2,1,0:T(8,128)(2,1)S(1)} all-to-all(s16[16,136,128]{2,1,0:T(8,128)(2,1)S(1)} %scan.2), channel_id=1, replica_groups=mesh['tm'=16,'space'=8] {'tm'}, dimensions={0} | all-to-all | bytes 1114112 | tf_op jit(solution)/shard_map/all_to_all | solution.py:513
  84.4 1.3 edges.1
  85.7 1.3 collective-permute-start.2
  87.0 1.5 %collective-permute-start.3 = (bf16[2,4,64,128]{3,2,1,0:T(8,128)(2,1)S(1)}, bf16[2,4,64,128]{3,2,1,0:T(8,128)(2,1)S(1)}, u32[]{:S(2)}, u32[]{:S(2)}) collective-permute-start(bf16[2,4,64,128]{3,2,1,0:T(8,128)(2,1)S(1)} %get-tuple-element.25), channel_id=1, source_target_pairs={{1,0},{2,1},{3,2},{4,3},{5,4},{6,5},{7,6},{9,8},{10,9},{11,10},{12... | collective-permute-start | bytes 393224 | tf_op jit(solution)/shard_map/ppermute | solution.py:518
  88.5 11.1 %inner2.1.in_hbm_ref = f32[2,4,4,64,128]{4,3,2,1,0:T(8,128)S(1)} custom-call(s32[2]{0:T(128)S(1)} %pad_add_fusion.rank_ref, s16[4,4,136,128]{3,2,1,0:T(8,128)(2,1)S(1)} %bitcast.14, f32[2,4,8,64,128]{4,3,2,1,0:T(8,128)} %traj_hbm.5, f32[4,8,64,128]{3,2,1,0:T(8,128)S(1)} %get-tuple-element.23.sum_ref.before_hbm, ...), custom_call_target="tpu_custom_call" | custom-call | tf_op jit(solution)/shard_map/inner2/pallas_call | solution.py:68
  99.7 0.0 collective-permute-done.2.lo_ref
  99.7 0.0 collective-permute-done.3.hi_ref
  99.7 12.6 %outer2.1 = (s16[4,4,136,128]{3,2,1,0:T(8,128)(2,1)S(1)}, f32[4,8,64,128]{3,2,1,0:T(8,128)S(1)}, f32[4,8,64,128]{3,2,1,0:T(8,128)S(1)}) custom-call(s32[2]{0:T(128)S(1)} %pad_add_fusion.rank_ref, s32[33]{0:T(128)S(1)} %copy-done.5, s16[4,4,136,128]{3,2,1,0:T(8,128)(2,1)S(1)} %bitcast.15, bf16[2,4,64,128]{3,2,1,0:T(8,128)(2,1)S(1)} %collective-permute-done.2.lo_ref, ...), custom_call_target="tpu_custom_call" | custom-call | tf_op jit(solution)/shard_map/outer2/pallas_call | solution.py:68
  112.3 16.1 %all_to_all.32.got_ref = s16[16,136,128]{2,1,0:T(8,128)(2,1)S(1)} all-to-all(s16[16,136,128]{2,1,0:T(8,128)(2,1)S(1)} %bitcast.17), channel_id=1, replica_groups=mesh['tm'=16,'space'=8] {'tm'}, dimensions={0} | all-to-all | bytes 1114112 | tf_op jit(solution)/shard_map/all_to_all | solution.py:511
  128.4 0.3 scan.3
  128.7 15.5 %all_to_all.33 = s16[16,136,128]{2,1,0:T(8,128)(2,1)S(1)} all-to-all(s16[16,136,128]{2,1,0:T(8,128)(2,1)S(1)} %scan.3), channel_id=1, replica_groups=mesh['tm'=16,'space'=8] {'tm'}, dimensions={0} | all-to-all | bytes 1114112 | tf_op jit(solution)/shard_map/all_to_all | solution.py:513
  144.3 2.0 %last_states.1 = f32[2,4,8,64,128]{4,3,2,1,0:T(8,128)} custom-call(s16[4,4,136,128]{3,2,1,0:T(8,128)(2,1)S(1)} %bitcast.16, f32[4,8,64,128]{3,2,1,0:T(8,128)S(1)} %get-tuple-element.27.sum0_ref, f32[4,8,64,128]{3,2,1,0:T(8,128)S(1)} %get-tuple-element.28.sum1_ref), custom_call_target="tpu_custom_call" | custom-call | tf_op jit(solution)/shard_map/last_states/pallas_call | solution.py:418
  (2 shorter events, 0.0 us)
Async XLA Ops:
  0.0 11.3 %copy-start = (bf16[128,128]{1,0:T(8,128)(2,1)S(1)}, bf16[128,128]{1,0:T(8,128)(2,1)}, u32[]{:S(2)}) copy-start(bf16[128,128]{1,0:T(8,128)(2,1)} %param.14) | copy-start | bytes 98308
  0.0 11.5 %copy-start.3 = (bf16[4,108,256]{2,1,0:T(8,128)(2,1)S(1)}, bf16[4,108,256]{2,1,0:T(8,128)(2,1)}, u32[]{:S(2)}) copy-start(bf16[4,108,256]{2,1,0:T(8,128)(2,1)} %constant.16.clone.sel_ref) | copy-start | bytes 663556
  0.0 11.1 %copy-start.5 = (s32[33]{0:T(128)S(1)}, s32[33]{0:T(128)}, u32[]{:S(2)}) copy-start(s32[33]{0:T(128)} %ts_ref.3) | copy-start | bytes 400
  0.0 11.5 %copy-start.6 = (bf16[4,128]{1,0:T(4,128)(2,1)S(1)}, bf16[4,128]{1,0:T(4,128)(2,1)}, u32[]{:S(2)}) copy-start(bf16[4,128]{1,0:T(4,128)(2,1)} %out_ref.1) | copy-start | bytes 3076
  0.0 11.5 %copy-start.4 = (bf16[128,108]{0,1:T(8,128)(2,1)S(1)}, bf16[128,108]{0,1:T(8,128)(2,1)}, u32[]{:S(2)}) copy-start(bf16[128,108]{0,1:T(8,128)(2,1)} %param.13) | copy-start | bytes 82948
  1.9 21.0 %all-to-all-start = ((f32[8,8,1024]{2,1,0:T(8,128)}), f32[8,8,1024]{2,1,0:T(8,128)S(1)}, u32[]{:S(2)}, u32[]{:S(2)}) async-start(f32[8,8,1024]{2,1,0:T(8,128)} %get-tuple-element.21), calls=%async_computation | async-start | bytes 524288 | tf_op jit(solution)/shard_map/all_to_all | solution.py:538
  7.4 15.6 %collective-permute-start = (bf16[2,4,64,128]{3,2,1,0:T(8,128)(2,1)S(1)}, bf16[2,4,64,128]{3,2,1,0:T(8,128)(2,1)S(1)}, u32[]{:S(2)}, u32[]{:S(2)}) collective-permute-start(bf16[2,4,64,128]{3,2,1,0:T(8,128)(2,1)S(1)} %get-tuple-element.19), channel_id=1, source_target_pairs={{0,1},{1,2},{2,3},{3,4},{4,5},{5,6},{6,7},{8,9},{9,10},{10,11},{11... | collective-permute-start | bytes 393224 | tf_op jit(solution)/shard_map/ppermute | solution.py:517
  9.8 13.2 %collective-permute-start.1 = (bf16[2,4,64,128]{3,2,1,0:T(8,128)(2,1)S(1)}, bf16[2,4,64,128]{3,2,1,0:T(8,128)(2,1)S(1)}, u32[]{:S(2)}, u32[]{:S(2)}) collective-permute-start(bf16[2,4,64,128]{3,2,1,0:T(8,128)(2,1)S(1)} %get-tuple-element.20), channel_id=1, source_target_pairs={{1,0},{2,1},{3,2},{4,3},{5,4},{6,5},{7,6},{9,8},{10,9},{11,10},{12... | collective-permute-start | bytes 393224 | tf_op jit(solution)/shard_map/ppermute | solution.py:518
  22.9 3.5 %copy-start.1 = (bf16[2,4,64,128]{3,2,1,0:T(8,128)(2,1)}, bf16[2,4,64,128]{3,2,1,0:T(8,128)(2,1)S(1)}, u32[]{:S(2)}) copy-start(bf16[2,4,64,128]{3,2,1,0:T(8,128)(2,1)S(1)} %collective-permute-done.1.hi_ref.refs_2_) | copy-start | bytes 393220
  26.5 20.2 %all-to-all-start.1 = ((s16[16,176,128]{2,1,0:T(8,128)(2,1)}), s16[16,176,128]{2,1,0:T(8,128)(2,1)S(1)}, u32[]{:S(2)}, u32[]{:S(2)}) async-start(s16[16,176,128]{2,1,0:T(8,128)(2,1)} %wells.1), calls=%async_computation.1 | async-start | bytes 1441792 | tf_op jit(solution)/shard_map/all_to_all | solution.py:551
  33.5 0.9 copy-start.2
  85.7 13.9 %collective-permute-start.2 = (bf16[2,4,64,128]{3,2,1,0:T(8,128)(2,1)S(1)}, bf16[2,4,64,128]{3,2,1,0:T(8,128)(2,1)S(1)}, u32[]{:S(2)}, u32[]{:S(2)}) collective-permute-start(bf16[2,4,64,128]{3,2,1,0:T(8,128)(2,1)S(1)} %get-tuple-element.24), channel_id=1, source_target_pairs={{0,1},{1,2},{2,3},{3,4},{4,5},{5,6},{6,7},{8,9},{9,10},{10,11},{11... | collective-permute-start | bytes 393224 | tf_op jit(solution)/shard_map/ppermute | solution.py:517
  87.0 12.6 %collective-permute-start.3 = (bf16[2,4,64,128]{3,2,1,0:T(8,128)(2,1)S(1)}, bf16[2,4,64,128]{3,2,1,0:T(8,128)(2,1)S(1)}, u32[]{:S(2)}, u32[]{:S(2)}) collective-permute-start(bf16[2,4,64,128]{3,2,1,0:T(8,128)(2,1)S(1)} %get-tuple-element.25), channel_id=1, source_target_pairs={{1,0},{2,1},{3,2},{4,3},{5,4},{6,5},{7,6},{9,8},{10,9},{11,10},{12... | collective-permute-start | bytes 393224 | tf_op jit(solution)/shard_map/ppermute | solution.py:518

commit v3 on v2

--- a/solution.py
+++ b/solution.py
@@ -18,7 +18,7 @@
 TIME_SCALE = 500.0
 EXP = 8
 PAY = 2 * NX + EXP
-GPAY = 5 * 32 + 16
+GROWS = 5 * NX + 16
 MIB = 2**20
 
 
@@ -175,9 +175,9 @@
     pltpu.VMEM((2, 512, 256), BF16),
     pltpu.VMEM(((NX + 9) * 40, NY), F32),
     pltpu.VMEM((2, (NX + 10) * 48, NY), BF16),
-    pltpu.VMEM((72 * 16, NY), F32),
-    pltpu.VMEM((4, 512, 256), BF16),
-    pltpu.VMEM((4, 512, 256), BF16),
+    pltpu.VMEM(((NX + 16) * 16, NY), F32),
+    pltpu.VMEM((8, 512, 256), BF16),
+    pltpu.VMEM((8, 512, 256), BF16),
 ]
 
 
@@ -212,8 +212,8 @@
     ones = jnp.ones((16, 256), BF16)
 
     def first(t, hidden):
-        for g in range(4):
-            xq, i = 2 * t + g // 2, g % 2
+        for g in range(8):
+            xq, i = 4 * t + g // 2, g % 2
             b0 = pl.multiple_of(xq * 192, 16)
             pa = Q[i, pl.ds(b0, 192), :]
             pb = Q[i, pl.ds(b0 + 96, 192), :]
@@ -221,16 +221,16 @@
             u = jnp.dot(wbig[:, 0:208], patch, preferred_element_type=F32)
             hidden[g] = (u + u * jnp.tanh(u)).astype(BF16)
             for k in range(2):
-                prep(8 * t + 9 + 2 * g + k)
+                prep(16 * t + 9 + 2 * g + k)
             yield
 
     def second(t, hidden):
-        for g in range(4):
-            xq, i = 2 * t + g // 2, g % 2
+        for g in range(8):
+            xq, i = 4 * t + g // 2, g % 2
             r = jnp.dot(w2_ref[...], hidden[g], preferred_element_type=F32)
             for hh in range(2):
                 for xx in range(2):
-                    st = pl.multiple_of((xq * 4 + 8 + 2 * hh + xx) * 16, 8)
+                    st = pl.multiple_of((xq * 4 + 16 + 2 * hh + xx) * 16, 8)
                     So[pl.ds(st + i * 8, 8), :] = r[xx * 8:xx * 8 + 8, hh * NY:hh * NY + NY]
             yield
 
@@ -241,13 +241,13 @@
             pass
         return carry
 
-    lax.fori_loop(0, NX // 16, body, 0)
-    for _ in second(NX // 8 - 1, HB):
+    lax.fori_loop(0, NX // 32, body, 0)
+    for _ in second(NX // 16 - 1, HB):
         pass
     for i in range(2):
         for dd in range(2):
             for c in range(C):
-                put(c, 2 * i + dd, So[pl.ds(128 + i * 8 + dd * 4 + c, NX, stride=16), :])
+                put(c, 2 * i + dd, So[pl.ds(256 + i * 8 + dd * 4 + c, NX, stride=16), :])
 
 
 def convolve(state, pairs, halo, w2_ref, put, loads, scratch):
@@ -312,12 +312,21 @@
     convolve(lambda j, c, d: s[j, c, d - 1], INNER, None, w2_ref, put, loads, scratch)
 
 
-def outer1_kernel(s_hbm, wbig_hbm, w2_ref, lo_ref, hi_ref, o_ref, s, sems, *scratch):
-    step = lambda j: [(s_hbm.at[j, :, 0:3], s.at[j, :, 0:3]), (s_hbm.at[j, :, 5:8], s.at[j, :, 3:6])]
-    loads = Loads(sems, step0=step(0), weights=[(wbig_hbm, scratch[0])], step1=step(1))
-    put = lambda j, c, i, v: o_ref.__setitem__((j, c, i), v)
-    state = lambda j, c, d: s[j, c, d if d < 3 else d - 2]
-    convolve(state, OUTER, (lo_ref, hi_ref), w2_ref, put, loads, scratch)
+def outer1_kernel(
+    rank_ref, ts_ref, lo_ref, hi_ref, w2_ref, s_hbm, wbig_hbm, in_hbm_ref, n_hbm, own_hbm, other_hbm,
+    pay_ref, sum_ref, s, in_ref, n_ref, g_ref, out_ref, sems, *scratch,
+):
+    layers = lambda j, lo, hi: (s_hbm.at[j, :, lo:hi], s.at[j, :, lo:hi])
+    step = lambda j: [layers(j, 0, 3), layers(j, 5, 8)]
+    loads = Loads(
+        sems, step0=step(0), weights=[(wbig_hbm, scratch[0])], step1=step(1),
+        late=[layers(0, 3, 5), layers(1, 3, 5), (n_hbm, n_ref), (own_hbm, g_ref.at[rank_ref[0] % 2]), (other_hbm, g_ref.at[1 - rank_ref[0] % 2]), (in_hbm_ref, in_ref)],
+    )
+    put = lambda j, c, i, v: out_ref.__setitem__((j, c, i), v)
+    convolve(given(s), OUTER, (lo_ref, hi_ref), w2_ref, put, loads, scratch)
+    loads.wait("late")
+    start = first_of(rank_ref, s.at[0])
+    increments(given(s), rank_ref, ts_ref, in_ref, out_ref, n_ref, g_ref, start, pay_ref, [sum_ref])
 
 
 def gains(rank_ref, ts_ref):
@@ -330,45 +339,6 @@
     return step, gain
 
 
-def increments1_kernel(rank_ref, ts_ref, s_ref, in_ref, out_ref, n_ref, g_ref, pay_ref, sum_ref):
-    step, gain = gains(rank_ref, ts_ref)
-    keep = jnp.where(rank_ref[0] == 0, 1.0, 0.0)
-    pair = pl.program_id(0)
-    is_inner = jnp.logical_or(pair == 1, pair == 2)
-    for c in range(C):
-        totals = []
-        for dd in range(2):
-            observed, count = guide_at(g_ref, dd, c)
-            total = keep * s_ref[0, c, dd]
-            for j in range(2):
-                drift = jnp.where(is_inner, in_ref[j, c, dd], out_ref[j, c, dd])
-                drift = drift + GUIDE_GAIN * (observed - count * s_ref[j, c, dd])
-                total = total + step[j] * drift + gain[j] * n_ref[j, c, dd].astype(F32)
-                if j == 0:
-                    sum_ref[c, dd] = total
-            totals.append(total)
-        encode(totals, lambda at, n, v: pay_ref.__setitem__((c, pl.ds(at, n), slice(None)), v))
-
-
-def increments1(ranks, timesteps, s, inner, outer, noise, guide):
-    pair = lambda place: pl.BlockSpec((2, C, 2, NX, NY), lambda p: (0, 0, place(p), 0, 0))
-    return pl.pallas_call(
-        increments1_kernel,
-        grid=(4,),
-        in_specs=[
-            smem(), smem(), pair(lambda p: p), pair(lambda p: p // 2), pair(lambda p: p // 2), pair(lambda p: p),
-            pl.BlockSpec((4, GPAY, NY), lambda p: (p, 0, 0)),
-        ],
-        out_specs=[
-            pl.BlockSpec((C, None, PAY, NY), lambda p: (0, p, 0, 0)),
-            pl.BlockSpec((C, 2, NX, NY), lambda p: (0, p, 0, 0)),
-        ],
-        out_shape=[shape(I16, C, 4, PAY, NY), shape(F32, C, ND, NX, NY)],
-        compiler_params=params(16),
-        name="increments1",
-    )(ranks, timesteps, s, inner, outer, noise, guide)
-
-
 def inner2_kernel(rank_ref, e_ref, traj_hbm, before_hbm, wbig_hbm, w2_ref, o_ref, traj, before, sems, *scratch):
     loads = Loads(
         sems, step0=[(traj_hbm.at[0, :, 1:7], traj.at[0, :, 1:7])], weights=[(wbig_hbm, scratch[0])],
@@ -380,12 +350,12 @@
 
 
 def outer2_kernel(
-    rank_ref, ts_ref, e_ref, lo_ref, hi_ref, w2_ref, traj_hbm, before_hbm, wbig_hbm, in_hbm_ref, n_hbm, g_hbm,
+    rank_ref, ts_ref, e_ref, lo_ref, hi_ref, w2_ref, traj_hbm, before_hbm, wbig_hbm, in_hbm_ref, n_hbm, own_hbm, other_hbm,
     pay_ref, sum0_ref, sum1_ref, traj, before, in_ref, n_ref, g_ref, out_ref, sems, *scratch,
 ):
     loads = Loads(
         sems, step0=[(traj_hbm.at[0:1], traj)], weights=[(wbig_hbm, scratch[0])], step1=[(before_hbm, before)],
-        late=[(n_hbm, n_ref), (g_hbm, g_ref), (in_hbm_ref, in_ref)],
+        late=[(n_hbm, n_ref), (own_hbm, g_ref.at[rank_ref[0] % 2]), (other_hbm, g_ref.at[1 - rank_ref[0] % 2]), (in_hbm_ref, in_ref)],
     )
     start = first_of(rank_ref, traj.at[0])
     state = arrived(e_ref, start, before)
@@ -427,32 +397,35 @@
 
 
 def wells_kernel(rank_ref, rows_ref, *refs):
-    o_ref = refs[-1]
-    me_tm, me_space = rank_ref[0], rank_ref[1]
-    line = lax.broadcasted_iota(jnp.int32, (32, ROWS), 0) + 32 * me_tm
-    column = lax.broadcasted_iota(jnp.int32, (NY, ROWS), 0)
-    total = jnp.zeros((13 * 32, NY), F32)
+    o_ref, total_ref = refs[-2:]
+    half, me_space = rank_ref[0] % 2, rank_ref[1]
+    line = lax.broadcasted_iota(jnp.int32, (HID, ROWS), 0)
+    column = lax.broadcasted_iota(jnp.int32, (2 * NY, ROWS), 0)
     for src in range(SPACE):
         owner = rows_ref[src, 0:1, :].astype(jnp.int32)
         cell = rows_ref[src, 1:2, :].astype(jnp.int32)
-        at_line = jnp.where(owner == me_space, cell >> 7, -1)
+        here = jnp.logical_and(owner == me_space, (cell >> 15) == half)
+        at_line = jnp.where(here, ((cell >> 13) & 3) * 32 + ((cell >> 7) & 31), -1)
         hit = jnp.where(line == at_line, 1.0, 0.0)
-        pieces = [hit]
+        pieces = [hit.astype(BF16)]
         for c in range(C):
             v = rows_ref[src, 2 + c:3 + c, :]
             v1 = v.astype(BF16).astype(F32)
-            v2 = (v - v1).astype(BF16).astype(F32)
-            v3 = v - v1 - v2
-            pieces += [hit * v1, hit * v2, hit * v3]
-        left = jnp.concatenate(pieces, 0).astype(BF16)
-        right = jnp.where(column == (cell & 127), 1.0, 0.0).astype(BF16)
-        total = total + lax.dot_general(left, right, (((1,), (1,)), ((), ())), preferred_element_type=F32)
-    observed = [total[at:at + 32] + total[at + 32:at + 64] + total[at + 64:at + 96] for at in range(32, 13 * 32, 96)]
-    power, factor = power_of(observed)
-    pieces = [jnp.round(v * factor) for v in observed] + [total[0:32], jnp.broadcast_to(power, (16, NY))]
-    coded = jnp.concatenate(pieces, 0).astype(jnp.int32).astype(I16)
-    for k in range(TM):
-        o_ref[k] = coded
+            pieces += [(hit * v1).astype(BF16), (hit * (v - v1)).astype(BF16)]
+        left = jnp.concatenate(pieces, 0)
+        right = jnp.where(column == ((cell >> 12) & 1) * NY + (cell & 127), 1.0, 0.0).astype(BF16)
+        part = lax.dot_general(left, right, (((1,), (1,)), ((), ())), preferred_element_type=F32)
+        total_ref[...] = part if src == 0 else total_ref[...] + part
+    for d in range(4):
+        term = lambda k: jnp.concatenate(
+            [total_ref[pl.ds(k * HID + 32 * d, 32), pl.ds(h * NY, NY)] for h in range(2)], 0
+        )
+        observed = [term(1 + 2 * c) + term(2 + 2 * c) for c in range(C)]
+        power, factor = power_of(observed)
+        for c in range(C):
+            o_ref[d, c * NX:(c + 1) * NX, :] = jnp.round(observed[c] * factor).astype(jnp.int32).astype(I16)
+        o_ref[d, C * NX:5 * NX, :] = term(0).astype(jnp.int32).astype(I16)
+        o_ref[d, 5 * NX:GROWS, :] = jnp.broadcast_to(power, (16, NY)).astype(jnp.int32).astype(I16)
 
 
 def wells(ranks, rows, *earlier):
@@ -460,20 +433,17 @@
         wells_kernel,
         grid=(1,),
         in_specs=[smem(), full(rows.shape)] + [pl.BlockSpec(memory_space=pl.ANY)] * len(earlier),
-        out_specs=full((TM, GPAY, NY)),
-        out_shape=shape(I16, TM, GPAY, NY),
-        compiler_params=params(12),
+        out_specs=full((4, GROWS, NY)),
+        out_shape=shape(I16, 4, GROWS, NY),
+        scratch_shapes=[pltpu.VMEM((9 * HID, 2 * NY), F32)],
+        compiler_params=params(24),
         name="wells",
     )(ranks, rows, *earlier)
 
 
 def guide_at(g_ref, d, c):
-    observed, count = [], []
-    for k in (2 * d, 2 * d + 1):
-        wide = lambda at, n: g_ref[k, pl.ds(at, n), :].astype(jnp.int32).astype(F32)
-        observed.append(wide(c * 32, 32) * jnp.exp2(wide(5 * 32, 16)[0:1]))
-        count.append(wide(4 * 32, 32))
-    return jnp.concatenate(observed, 0), jnp.concatenate(count, 0)
+    wide = lambda at, n: g_ref[d // 4, d % 4, pl.ds(at, n), :].astype(jnp.int32).astype(F32)
+    return wide(c * NX, NX) * jnp.exp2(wide(5 * NX, 16)[0:1]), wide(C * NX, NX)
 
 
 def power_of(planes):
@@ -546,25 +516,27 @@
     six = vm(2, C, 6, NX, NY)
     sems = lambda n: pltpu.SemaphoreType.DMA((n,))
     s, wbig = Hbm(trajectory), Anywhere(wbig)
-    part = call(inner1_kernel, "inner1", 20, half, [], s, wbig, w2, scratch=[six, sems(3)] + CONV_SCRATCH)
-    guide = wells(ranks, rows, part, lo, hi)
-    guide = lax.all_to_all(guide, "tm", 0, 0, tiled=True)
-    rest = call(outer1_kernel, "outer1", 20, half, [], s, wbig, w2, lo, hi, scratch=[six, sems(5)] + CONV_SCRATCH)
-    payload, sums = increments1(ranks, timesteps, s.value, part, rest, in_hbm(noise), guide)
+    guide = wells(ranks, rows, lo, hi, wbig.value)
+    guide = [Anywhere(guide), Anywhere(lax.ppermute(guide, "tm", [(i, i ^ 1) for i in range(TM)]))]
+    part = call(inner1_kernel, "inner1", 24, half, [], s, wbig, w2, scratch=[six, sems(3)] + CONV_SCRATCH)
+    mine = [vm(*half.shape), pltpu.VMEM((2, C, ND, NX, NY), BF16), pltpu.VMEM((2, 4, GROWS, NY), I16), vm(*half.shape)]
+    payload, sums = call(
+        outer1_kernel, "outer1", 34, [coded, whole], [ranks, timesteps],
+        lo, hi, w2, s, wbig, Anywhere(part), Hbm(noise), *guide,
+        scratch=[vm(2, C, ND, NX, NY)] + mine + [sems(11)] + CONV_SCRATCH,
+    )
     entering = prefix(payload)
     lo, hi = halos(*call(edges_kernel, "edges", 8, [edge, edge], [ranks], entering, First(trajectory), sums))
     sums = Anywhere(sums)
     part = call(
-        inner2_kernel, "inner2", 20, half, [ranks], entering, s, sums, wbig, w2,
+        inner2_kernel, "inner2", 24, half, [ranks], entering, s, sums, wbig, w2,
         scratch=[vm(1, C, ND, NX, NY), vm(C, ND, NX, NY), sems(3)] + CONV_SCRATCH,
     )
     payload, sum0, sum1 = call(
-        outer2_kernel, "outer2", 32, [coded, whole, whole], [ranks, timesteps],
-        entering, lo, hi, w2, s, sums, wbig, Anywhere(part), Hbm(noise), Anywhere(guide),
+        outer2_kernel, "outer2", 36, [coded, whole, whole], [ranks, timesteps],
+        entering, lo, hi, w2, s, sums, wbig, Anywhere(part), Hbm(noise), *guide,
         scratch=[
-            vm(1, C, ND, NX, NY), vm(C, ND, NX, NY), vm(*half.shape), pltpu.VMEM((2, C, ND, NX, NY), BF16),
-            pltpu.VMEM((TM, GPAY, NY), I16), vm(*half.shape), sems(6),
-        ] + CONV_SCRATCH,
+            vm(1, C, ND, NX, NY), vm(C, ND, NX, NY)] + mine + [sems(7)] + CONV_SCRATCH,
     )
     return last_states(prefix(payload), sum0, sum1)
 

time: 147 us -> 143 us (0.973)
  starting transfers between devices: 18.9 us -> 14 us
    all_to_all x1 -> x0, starting transfers between devices: 7.03 us -> none  [per_device(): guide = lax.all_to_all(guide, 'tm', 0, 0, tiled=True)]
    pallas_call x1 -> x0, Pallas kernels: 3.56 us -> none  [increments1(): pl.pallas_call(increments1_kernel, grid=(4,), in_specs=[smem(), smem(), p...]
    pallas_call x1, Pallas kernels: 3.53 us -> 5.78 us  [wells(): pl.pallas_call(wells_kernel, grid=(1,), in_specs=[smem(), full(rows.shape...]
    ppermute x0 -> x1, starting transfers between devices: none -> 1.84 us  [per_device(): lax.ppermute(guide, 'tm', [(i, i ^ 1) for i in range(TM)])]
    ppermute x2, waiting for transfers between devices: 0.01 us -> 1.78 us  [halos(): hi = lax.ppermute(top, 'space', [(i + 1, i) for i in range(SPACE - 1)])]
    all_to_all x1 -> x0, waiting for transfers between devices: 1.76 us -> none  [per_device(): guide = lax.all_to_all(guide, 'tm', 0, 0, tiled=True)]
    all_to_all x2, blocking collectives: 31.1 us -> 32.8 us  [prefix(): return lax.all_to_all(ahead, 'tm', 0, 0, tiled=True).reshape(C, 4, PAY, NY)]
  transfers between devices with their start and end apart: 6 -> 6, of which waited for: 1 -> 2; matrix products, arithmetic and copies ran while one was open for 0% -> 0% of each run, Pallas kernels for 23% -> 16%
where the time goes in v3:
time: 143 us; the launch traced here: 141 us
  blocking collectives  66 us (46%)
  Pallas kernels  57.9 us (40%)
  starting transfers between devices  14 us (10%)
  waiting for transfers between devices  2.54 us (2%)
    pallas_call x8, Pallas kernels, call(): pl.pallas_call(kernel, grid=(1,), in_specs=[smem()] * len(scalars) + [spe...  48.1 us
    all_to_all x2, blocking collectives, prefix(): got = lax.all_to_all(payload.reshape(TM, PAY, NY), 'tm', 0, 0, tiled=True)  33.3 us
    all_to_all x2, blocking collectives, prefix(): return lax.all_to_all(ahead, 'tm', 0, 0, tiled=True).reshape(C, 4, PAY, NY)  32.8 us
    pallas_call x1, Pallas kernels, wells(): pl.pallas_call(wells_kernel, grid=(1,), in_specs=[smem(), full(rows.shape...  5.78 us
    all_to_all x1, starting transfers between devices, per_device(): rows = lax.all_to_all(rows, 'space', 0, 0, tiled=True)  5.43 us
    ppermute x2, starting transfers between devices, halos(): lo = lax.ppermute(bottom, 'space', [(i, i + 1) for i in range(SPACE - 1)])  3.88 us
  transfers between devices with their start and end apart: 6, of which 2 were waited for; matrix products, arithmetic and copies ran while one was open for 0% of the time, Pallas kernels for 16%

profile of v3, /device:TPU:0, one launch (start us, length us, event | category | flops | bytes accessed | tf_op | source)
XLA Modules:
  0.0 141.0 jit_solution(13544495429799870671)
XLA Ops:
  0.0 0.0 copy-start
  0.0 0.0 copy-start.1
  0.0 0.0 copy-start.3
  0.0 0.0 copy-start.4
  0.0 0.0 copy-start.2
  0.0 1.9 %pack.1 = (f32[8,8,1024]{2,1,0:T(8,128)}, bf16[2,4,64,128]{3,2,1,0:T(8,128)(2,1)S(1)}, bf16[2,4,64,128]{3,2,1,0:T(8,128)(2,1)S(1)}) custom-call(s32[1,1024]{1,0:T(1,128)} %bitcast.21, s32[1,1024]{1,0:T(1,128)} %bitcast.22, f32[4,1024]{1,0:T(4,128)} %bitcast.20, f32[2,4,8,64,128]{4,3,2,1,0:T(8,128)} %traj_hbm.5), custom_call_target="tpu_custom_call" | custom-call | tf_op jit(solution)/shard_map/pack/pallas_call | solution.py:136
  1.9 5.4 %all-to-all-start = ((f32[8,8,1024]{2,1,0:T(8,128)}), f32[8,8,1024]{2,1,0:T(8,128)S(1)}, u32[]{:S(2)}, u32[]{:S(2)}) async-start(f32[8,8,1024]{2,1,0:T(8,128)} %get-tuple-element.21), calls=%async_computation | async-start | bytes 524288 | tf_op jit(solution)/shard_map/all_to_all | solution.py:508
  7.4 2.4 %collective-permute-start = (bf16[2,4,64,128]{3,2,1,0:T(8,128)(2,1)S(1)}, bf16[2,4,64,128]{3,2,1,0:T(8,128)(2,1)S(1)}, u32[]{:S(2)}, u32[]{:S(2)}) collective-permute-start(bf16[2,4,64,128]{3,2,1,0:T(8,128)(2,1)S(1)} %get-tuple-element.17), channel_id=1, source_target_pairs={{0,1},{1,2},{2,3},{3,4},{4,5},{5,6},{6,7},{8,9},{9,10},{10,11},{11... | collective-permute-start | bytes 393224 | tf_op jit(solution)/shard_map/ppermute | solution.py:487
  9.8 1.3 collective-permute-start.1
  11.1 0.0 copy-done.3
  11.1 0.1 fusion
  11.3 0.0 copy-done
  11.3 0.2 convolution_bitcast_fusion.bias_ref
  11.5 0.1 pad_add_fusion.rank_ref
  11.5 0.0 copy-done.1
  11.5 0.0 copy-done.4
  11.5 0.0 copy-done.2
  11.5 0.8 weights.1
  12.4 0.0 collective-permute-done.refs_0_.lo_ref
  12.4 1.8 %collective-permute-done.1.refs_1_.hi_ref = bf16[2,4,64,128]{3,2,1,0:T(8,128)(2,1)S(1)} collective-permute-done((bf16[2,4,64,128]{3,2,1,0:T(8,128)(2,1)S(1)}, bf16[2,4,64,128]{3,2,1,0:T(8,128)(2,1)S(1)}, u32[]{:S(2)}, u32[]{:S(2)}) %collective-permute-start.1) | collective-permute-done | bytes 131104 | tf_op jit(solution)/shard_map/ppermute | solution.py:488
  14.1 0.8 all-to-all-done.rows_ref
  14.9 5.8 %wells.1.own_hbm = s16[4,336,128]{2,1,0:T(8,128)(2,1)S(1)} custom-call(s32[2]{0:T(128)S(1)} %pad_add_fusion.rank_ref, f32[8,8,1024]{2,1,0:T(8,128)S(1)} %all-to-all-done.rows_ref, bf16[2,4,64,128]{3,2,1,0:T(8,128)(2,1)S(1)} %collective-permute-done.refs_0_.lo_ref, bf16[2,4,64,128]{3,2,1,0:T(8,128)(2,1)S(1)} %collective-permute-done.1.refs_1_.hi_ref, ...), custom_call_target="tpu_custom_call" | custom-call | tf_op jit(solution)/shard_map/wells/pallas_call | solution.py:432
  20.7 1.8 %collective-permute-start.2 = (s16[4,336,128]{2,1,0:T(8,128)(2,1)S(1)}, s16[4,336,128]{2,1,0:T(8,128)(2,1)S(1)}, u32[]{:S(2)}, u32[]{:S(2)}) collective-permute-start(s16[4,336,128]{2,1,0:T(8,128)(2,1)S(1)} %wells.1.own_hbm), channel_id=1, source_target_pairs={{0,8},{8,0},{16,24},{24,16},{32,40},{40,32},{48,56},{56,48},{64,72... | collective-permute-start | bytes 1032200 | tf_op jit(solution)/shard_map/ppermute | solution.py:520
  22.5 10.2 %inner1.1.in_hbm_ref = f32[2,4,4,64,128]{4,3,2,1,0:T(8,128)S(1)} custom-call(f32[2,4,8,64,128]{4,3,2,1,0:T(8,128)} %traj_hbm.5, bf16[2,512,256]{2,1,0:T(8,128)(2,1)S(1)} %get-tuple-element.20.wbig_hbm.refs_2_, bf16[16,512]{1,0:T(8,128)(2,1)S(1)} %get-tuple-element.19.w2_ref), custom_call_target="tpu_custom_call" | custom-call | tf_op jit(solution)/shard_map/inner1/pallas_call | solution.py:68
  32.7 0.0 collective-permute-done.2.other_hbm
  32.7 12.0 %outer1.1 = (s16[4,4,136,128]{3,2,1,0:T(8,128)(2,1)S(1)}, f32[4,8,64,128]{3,2,1,0:T(8,128)S(1)}) custom-call(s32[2]{0:T(128)S(1)} %pad_add_fusion.rank_ref, s32[33]{0:T(128)S(1)} %copy-done.3, bf16[2,4,64,128]{3,2,1,0:T(8,128)(2,1)S(1)} %collective-permute-done.refs_0_.lo_ref, bf16[2,4,64,128]{3,2,1,0:T(8,128)(2,1)S(1)} %collective-permute-done.1.refs_1_.hi_ref, ...), custom_call_target="tpu_custom_call" | custom-call | tf_op jit(solution)/shard_map/outer1/pallas_call | solution.py:68
  44.7 18.9 %all_to_all.25.got_ref = s16[16,136,128]{2,1,0:T(8,128)(2,1)S(1)} all-to-all(s16[16,136,128]{2,1,0:T(8,128)(2,1)S(1)} %bitcast.18), channel_id=1, replica_groups=mesh['tm'=16,'space'=8] {'tm'}, dimensions={0} | all-to-all | bytes 1114112 | tf_op jit(solution)/shard_map/all_to_all | solution.py:481
  63.6 0.3 scan.2
  63.9 16.2 %all_to_all.26 = s16[16,136,128]{2,1,0:T(8,128)(2,1)S(1)} all-to-all(s16[16,136,128]{2,1,0:T(8,128)(2,1)S(1)} %scan.2), channel_id=1, replica_groups=mesh['tm'=16,'space'=8] {'tm'}, dimensions={0} | all-to-all | bytes 1114112 | tf_op jit(solution)/shard_map/all_to_all | solution.py:483
  80.1 1.3 edges.1
  81.4 1.5 %collective-permute-start.3 = (bf16[2,4,64,128]{3,2,1,0:T(8,128)(2,1)S(1)}, bf16[2,4,64,128]{3,2,1,0:T(8,128)(2,1)S(1)}, u32[]{:S(2)}, u32[]{:S(2)}) collective-permute-start(bf16[2,4,64,128]{3,2,1,0:T(8,128)(2,1)S(1)} %get-tuple-element.24), channel_id=1, source_target_pairs={{0,1},{1,2},{2,3},{3,4},{4,5},{5,6},{6,7},{8,9},{9,10},{10,11},{11... | collective-permute-start | bytes 393224 | tf_op jit(solution)/shard_map/ppermute | solution.py:487
  82.9 1.5 %collective-permute-start.4 = (bf16[2,4,64,128]{3,2,1,0:T(8,128)(2,1)S(1)}, bf16[2,4,64,128]{3,2,1,0:T(8,128)(2,1)S(1)}, u32[]{:S(2)}, u32[]{:S(2)}) collective-permute-start(bf16[2,4,64,128]{3,2,1,0:T(8,128)(2,1)S(1)} %get-tuple-element.25), channel_id=1, source_target_pairs={{1,0},{2,1},{3,2},{4,3},{5,4},{6,5},{7,6},{9,8},{10,9},{11,10},{12... | collective-permute-start | bytes 393224 | tf_op jit(solution)/shard_map/ppermute | solution.py:488
  84.5 10.9 %inner2.1.in_hbm_ref = f32[2,4,4,64,128]{4,3,2,1,0:T(8,128)S(1)} custom-call(s32[2]{0:T(128)S(1)} %pad_add_fusion.rank_ref, s16[4,4,136,128]{3,2,1,0:T(8,128)(2,1)S(1)} %bitcast.14, f32[2,4,8,64,128]{4,3,2,1,0:T(8,128)} %traj_hbm.5, f32[4,8,64,128]{3,2,1,0:T(8,128)S(1)} %get-tuple-element.23.sum_ref.before_hbm, ...), custom_call_target="tpu_custom_call" | custom-call | tf_op jit(solution)/shard_map/inner2/pallas_call | solution.py:68
  95.4 0.0 collective-permute-done.3.lo_ref
  95.4 0.0 collective-permute-done.4.hi_ref
  95.4 12.3 %outer2.1 = (s16[4,4,136,128]{3,2,1,0:T(8,128)(2,1)S(1)}, f32[4,8,64,128]{3,2,1,0:T(8,128)S(1)}, f32[4,8,64,128]{3,2,1,0:T(8,128)S(1)}) custom-call(s32[2]{0:T(128)S(1)} %pad_add_fusion.rank_ref, s32[33]{0:T(128)S(1)} %copy-done.3, s16[4,4,136,128]{3,2,1,0:T(8,128)(2,1)S(1)} %bitcast.15, bf16[2,4,64,128]{3,2,1,0:T(8,128)(2,1)S(1)} %collective-permute-done.3.lo_ref, ...), custom_call_target="tpu_custom_call" | custom-call | tf_op jit(solution)/shard_map/outer2/pallas_call | solution.py:68
  107.7 14.4 %all_to_all.27.got_ref = s16[16,136,128]{2,1,0:T(8,128)(2,1)S(1)} all-to-all(s16[16,136,128]{2,1,0:T(8,128)(2,1)S(1)} %bitcast.17), channel_id=1, replica_groups=mesh['tm'=16,'space'=8] {'tm'}, dimensions={0} | all-to-all | bytes 1114112 | tf_op jit(solution)/shard_map/all_to_all | solution.py:481
  122.1 0.3 scan.3
  122.4 16.6 %all_to_all.28 = s16[16,136,128]{2,1,0:T(8,128)(2,1)S(1)} all-to-all(s16[16,136,128]{2,1,0:T(8,128)(2,1)S(1)} %scan.3), channel_id=1, replica_groups=mesh['tm'=16,'space'=8] {'tm'}, dimensions={0} | all-to-all | bytes 1114112 | tf_op jit(solution)/shard_map/all_to_all | solution.py:483
  139.0 2.0 %last_states.1 = f32[2,4,8,64,128]{4,3,2,1,0:T(8,128)} custom-call(s16[4,4,136,128]{3,2,1,0:T(8,128)(2,1)S(1)} %bitcast.16, f32[4,8,64,128]{3,2,1,0:T(8,128)S(1)} %get-tuple-element.27.sum0_ref, f32[4,8,64,128]{3,2,1,0:T(8,128)S(1)} %get-tuple-element.28.sum1_ref), custom_call_target="tpu_custom_call" | custom-call | tf_op jit(solution)/shard_map/last_states/pallas_call | solution.py:388
  (2 shorter events, 0.0 us)
Async XLA Ops:
  0.0 11.3 %copy-start = (bf16[128,128]{1,0:T(8,128)(2,1)S(1)}, bf16[128,128]{1,0:T(8,128)(2,1)}, u32[]{:S(2)}) copy-start(bf16[128,128]{1,0:T(8,128)(2,1)} %param.14) | copy-start | bytes 98308
  0.0 11.5 %copy-start.1 = (bf16[4,108,256]{2,1,0:T(8,128)(2,1)S(1)}, bf16[4,108,256]{2,1,0:T(8,128)(2,1)}, u32[]{:S(2)}) copy-start(bf16[4,108,256]{2,1,0:T(8,128)(2,1)} %constant.16.clone.sel_ref) | copy-start | bytes 663556
  0.0 11.1 %copy-start.3 = (s32[33]{0:T(128)S(1)}, s32[33]{0:T(128)}, u32[]{:S(2)}) copy-start(s32[33]{0:T(128)} %ts_ref.3) | copy-start | bytes 400
  0.0 11.5 %copy-start.4 = (bf16[4,128]{1,0:T(4,128)(2,1)S(1)}, bf16[4,128]{1,0:T(4,128)(2,1)}, u32[]{:S(2)}) copy-start(bf16[4,128]{1,0:T(4,128)(2,1)} %out_ref.1) | copy-start | bytes 3076
  0.0 11.5 %copy-start.2 = (bf16[128,108]{0,1:T(8,128)(2,1)S(1)}, bf16[128,108]{0,1:T(8,128)(2,1)}, u32[]{:S(2)}) copy-start(bf16[128,108]{0,1:T(8,128)(2,1)} %param.13) | copy-start | bytes 82948
  1.9 13.0 %all-to-all-start = ((f32[8,8,1024]{2,1,0:T(8,128)}), f32[8,8,1024]{2,1,0:T(8,128)S(1)}, u32[]{:S(2)}, u32[]{:S(2)}) async-start(f32[8,8,1024]{2,1,0:T(8,128)} %get-tuple-element.21), calls=%async_computation | async-start | bytes 524288 | tf_op jit(solution)/shard_map/all_to_all | solution.py:508
  7.4 5.0 %collective-permute-start = (bf16[2,4,64,128]{3,2,1,0:T(8,128)(2,1)S(1)}, bf16[2,4,64,128]{3,2,1,0:T(8,128)(2,1)S(1)}, u32[]{:S(2)}, u32[]{:S(2)}) collective-permute-start(bf16[2,4,64,128]{3,2,1,0:T(8,128)(2,1)S(1)} %get-tuple-element.17), channel_id=1, source_target_pairs={{0,1},{1,2},{2,3},{3,4},{4,5},{5,6},{6,7},{8,9},{9,10},{10,11},{11... | collective-permute-start | bytes 393224 | tf_op jit(solution)/shard_map/ppermute | solution.py:487
  9.8 4.4 %collective-permute-start.1 = (bf16[2,4,64,128]{3,2,1,0:T(8,128)(2,1)S(1)}, bf16[2,4,64,128]{3,2,1,0:T(8,128)(2,1)S(1)}, u32[]{:S(2)}, u32[]{:S(2)}) collective-permute-start(bf16[2,4,64,128]{3,2,1,0:T(8,128)(2,1)S(1)} %get-tuple-element.18), channel_id=1, source_target_pairs={{1,0},{2,1},{3,2},{4,3},{5,4},{6,5},{7,6},{9,8},{10,9},{11,10},{12... | collective-permute-start | bytes 393224 | tf_op jit(solution)/shard_map/ppermute | solution.py:488
  20.7 12.1 %collective-permute-start.2 = (s16[4,336,128]{2,1,0:T(8,128)(2,1)S(1)}, s16[4,336,128]{2,1,0:T(8,128)(2,1)S(1)}, u32[]{:S(2)}, u32[]{:S(2)}) collective-permute-start(s16[4,336,128]{2,1,0:T(8,128)(2,1)S(1)} %wells.1.own_hbm), channel_id=1, source_target_pairs={{0,8},{8,0},{16,24},{24,16},{32,40},{40,32},{48,56},{56,48},{64,72... | collective-permute-start | bytes 1032200 | tf_op jit(solution)/shard_map/ppermute | solution.py:520
  81.4 13.9 %collective-permute-start.3 = (bf16[2,4,64,128]{3,2,1,0:T(8,128)(2,1)S(1)}, bf16[2,4,64,128]{3,2,1,0:T(8,128)(2,1)S(1)}, u32[]{:S(2)}, u32[]{:S(2)}) collective-permute-start(bf16[2,4,64,128]{3,2,1,0:T(8,128)(2,1)S(1)} %get-tuple-element.24), channel_id=1, source_target_pairs={{0,1},{1,2},{2,3},{3,4},{4,5},{5,6},{6,7},{8,9},{9,10},{10,11},{11... | collective-permute-start | bytes 393224 | tf_op jit(solution)/shard_map/ppermute | solution.py:487
  82.9 12.4 %collective-permute-start.4 = (bf16[2,4,64,128]{3,2,1,0:T(8,128)(2,1)S(1)}, bf16[2,4,64,128]{3,2,1,0:T(8,128)(2,1)S(1)}, u32[]{:S(2)}, u32[]{:S(2)}) collective-permute-start(bf16[2,4,64,128]{3,2,1,0:T(8,128)(2,1)S(1)} %get-tuple-element.25), channel_id=1, source_target_pairs={{1,0},{2,1},{3,2},{4,3},{5,4},{6,5},{7,6},{9,8},{10,9},{11,10},{12... | collective-permute-start | bytes 393224 | tf_op jit(solution)/shard_map/ppermute | solution.py:488
